TPU v7x, 256 devices: a whole 4x4x8 slice. The times are simulated.
256 devices in a mesh: group: 16 (over z, core), member: 16 (over x, y).
Axes of the slice: x: 4, y: 4, z: 8, core: 2. Of those that a mesh axis runs over, the one named last changes fastest.
Arguments:
- features: float32 [98304, 256], P(('group', 'member')), may hold values from 0.01 to 9
- tiles: float32 [24576, 128, 128], P(('group', 'member')), may hold values from 0 to 1.5, as said below
- tile_col: int32 [24576], P(('group', 'member')), may hold values from 0 to 47
- tile_slot: int32 [24576], P(('group', 'member')), may hold values from 0 to 31
- mirror_list: int32 [256, 16, 2], P(('group', 'member')), may hold values from 0 to 2, as said below
- tile_counts: int32 [256], P(('group', 'member')), may hold values from 64 to 96, as said below
- self_weight: float32 [2, 256, 256], replicated, may hold values from -0.375 to 0.375
- neigh_weight: float32 [2, 256, 256], replicated, may hold values from -0.375 to 0.375
Outputs:
- embeddings: float32 [98304, 256], P(('group', 'member'))
Inputs may be any that keep to these rules, and one draw needn't show every extreme that they name: `tiles`: positive edge weights. `tile_col`: an index among the 48 blocks of the tile's group. `tile_slot`: an index among the device's 32 mirror slots. `mirror_list`: the 2 entries of one device and one destination group differ. `tile_counts`: some device has all 96 tiles live.
All inputs are finite; a program needn't handle non-finite values.
Results may differ from a plain program's by a relative error of at most 0.0003.
Values sent between devices are 32-bit elements; how exact they have to be, the bound alone decides.
No kernel may reach another device: no remote copies, remote signals or barrier semaphores. Data moves between devices by JAX's collectives and lax.ppermute only.
A program may use at most 128 MiB of HBM per device.

v0:
```python
import functools

import jax
import jax.numpy as jnp
from jax import lax
from jax.experimental import pallas as pl
from jax.experimental.pallas import tpu as pltpu
from jax.sharding import Mesh
from jax.sharding import PartitionSpec as P

F = 256
TILE = 128
LAYERS = 2
BLK_DEV = 3
TILES_DEV = 96
CAP = 2
NZ, NC, NX, NY = 8, 2, 4, 4
AXES = ("z", "c", "x", "y")
UNROLL = 8
PIECES = (2, 2, 4)
BASE = (0, 4, 8)
SEGMENTS = len(PIECES)
SLOTS = 2 * TILES_DEV + SEGMENTS * UNROLL
SOURCE, DEST, BOUNDS = SLOTS, 2 * SLOTS, 3 * SLOTS
LISTED = 3 * SLOTS + 8
ROWS = BLK_DEV * TILE
NT = (((1,), (1,)), ((), ()))
BF = jnp.bfloat16
F32 = jnp.float32
VMEM = pl.BlockSpec(memory_space=pltpu.VMEM)
SMEM = pl.BlockSpec(memory_space=pltpu.SMEM)


def perm(step):
    pairs = []
    for z in range(NZ):
        for c in range(NC):
            for x in range(NX):
                for y in range(NY):
                    tz, tc, tx, ty = step(z, c, x, y)
                    pairs.append((
                        ((z * NC + c) * NX + x) * NY + y,
                        (((tz % NZ) * NC + tc % NC) * NX + tx % NX) * NY + ty % NY,
                    ))
    return pairs


PAIR = perm(lambda z, c, x, y: (z, c + 1, x, y))


def along_z(d):
    return perm(lambda z, c, x, y: (z + (d if c == 0 else -d), c, x, y))


def in_plane(d, phase):
    return perm(lambda z, c, x, y: (z, c, x + d, y) if (c + phase) % 2 == 0 else (z, c, x, y + d))


def send(value, pairs):
    return lax.ppermute(value, AXES, pairs)


def split(value):
    high = value.astype(BF)
    return high, (value - high.astype(F32)).astype(BF)


def slot_of(offset):
    return jnp.where(offset == 0, 0, jnp.where(offset == 3, 1, jnp.where(offset == 1, 2, 3)))


def piece_of(r):
    return jnp.where(
        r == 3, 0, jnp.where(r == 6, 1, jnp.where(r == 2, 0, jnp.where(r == 7, 1, jnp.where(r == 1, 2, 3))))
    )


def plan_kernel(place, col, slot, mirror, count, listed, cls, nxt):
    z, c, p, q = place[0], place[1], place[2], place[3]
    for s in range(SEGMENTS + 1):
        nxt[s] = 0

    def classify(t, _):
        sl = slot[t]
        g = sl // CAP
        gz, gc = g // NC, g % NC
        r = lax.bitwise_and(jnp.where(gc == 0, gz - z, z - gz) + NZ, NZ - 1)
        first = jnp.logical_or(r == 4, r == 5)
        second = jnp.logical_or(r == 3, r == 6)
        seg = jnp.where(first, 0, jnp.where(second, 1, 2))
        piece = jnp.where(first, r - 4, piece_of(r)) + BASE[1] * seg
        piece += jnp.where(gc == c, jnp.where(seg == 2, PIECES[2], PIECES[0]), 0)
        seg = jnp.where(t < count[0], seg, SEGMENTS)
        cls[t] = seg * 64 + piece * 4 + mirror[sl]
        nxt[seg] = nxt[seg] + 1
        return 0

    lax.fori_loop(0, TILES_DEV, classify, 0)
    start = jnp.int32(0)
    for s in range(SEGMENTS):
        n = nxt[s]
        end = start + (n + UNROLL - 1) // UNROLL * UNROLL
        listed[BOUNDS + s] = start // UNROLL
        nxt[s] = start

        def pad(at, _):
            listed[at] = TILES_DEV
            listed[SOURCE + at] = 0
            listed[DEST + at] = 0
            return 0

        lax.fori_loop(start + n, end, pad, 0)
        start = end
    listed[BOUNDS + SEGMENTS] = start // UNROLL
    nxt[SEGMENTS] = start

    def place_tile(t, _):
        v = cls[t]
        seg = v // 64
        at = nxt[seg]
        nxt[seg] = at + 1
        b = col[t]
        m = b // BLK_DEV
        j = b - m * BLK_DEV
        bx, by = m // NY, m % NY
        sp = slot_of(lax.bitwise_and(jnp.where(c == 0, bx, by) - p + 4, 3))
        sq = slot_of(lax.bitwise_and(jnp.where(c == 0, by, bx) - q + 4, 3))
        listed[at] = t
        listed[SOURCE + at] = sq * 12 + sp * 3 + j
        listed[DEST + at] = v - seg * 64
        return 0

    lax.fori_loop(0, TILES_DEV, place_tile, 0)


def plan(place, col, slot, mirror, count):
    return pl.pallas_call(
        plan_kernel,
        out_shape=jax.ShapeDtypeStruct((LISTED,), jnp.int32),
        in_specs=[SMEM] * 5,
        out_specs=SMEM,
        scratch_shapes=[pltpu.SMEM((TILES_DEV,), jnp.int32), pltpu.SMEM((8,), jnp.int32)],
        cost_estimate=pl.CostEstimate(flops=0, bytes_accessed=2 * 10**7, transcendentals=0),
        name="plan",
    )(place, col, slot, mirror, count)


def tile_at(listed, tiles, s):
    t = listed[s]
    live = (t < TILES_DEV).astype(F32)
    return split(tiles[jnp.minimum(t, TILES_DEV - 1)] * live)


def degree_kernel(listed, tiles, degree):
    degree[...] = jnp.zeros_like(degree)
    ones = jnp.ones((8, TILE), BF)

    def chunk(i, _):
        for u in range(UNROLL):
            s = i * UNROLL + u
            hi, lo = tile_at(listed, tiles, s)
            row = lax.dot_general(ones, hi, NT, preferred_element_type=F32) + lax.dot_general(
                ones, lo, NT, preferred_element_type=F32
            )
            d = listed[DEST + s]
            degree[d // 4, pl.ds(d % 4, 1), :] += row[0:1]
        return 0

    lax.fori_loop(0, listed[BOUNDS + SEGMENTS], chunk, 0)


def degrees(listed, tiles):
    return pl.pallas_call(
        degree_kernel,
        out_shape=jax.ShapeDtypeStruct((2 * NZ, 8, TILE), F32),
        in_specs=[SMEM, VMEM],
        out_specs=VMEM,
        compiler_params=pltpu.CompilerParams(vmem_limit_bytes=16 << 20),
        cost_estimate=pl.CostEstimate(flops=10**8, bytes_accessed=2 * 10**7, transcendentals=0),
        name="degrees",
    )(listed, tiles)


def add_products(stage, rows, listed, tiles, degree, high, low, out):
    places, base = out.shape[0], BASE[stage]

    def clear(i, _):
        out[i] = jnp.zeros((rows, F), F32)
        if rows > ROWS:
            out[i, ROWS:rows, 0:TILE] = degree[base + i]
        return 0

    lax.fori_loop(0, places, clear, 0)

    def chunk(i, _):
        for u in range(UNROLL):
            s = i * UNROLL + u
            b = listed[SOURCE + s]
            hi, lo = tile_at(listed, tiles, s)
            value = jnp.dot(
                jnp.concatenate([hi, lo, hi], axis=1),
                jnp.concatenate([high[b], high[b], low[b]], axis=0),
                preferred_element_type=F32,
            )
            d = listed[DEST + s]
            at = pl.ds(pl.multiple_of(d % 4 * TILE, TILE), TILE)
            out[jnp.maximum(d // 4 - base, 0), at, :] += value
        return 0

    lax.fori_loop(listed[BOUNDS + stage], listed[BOUNDS + stage + 1], chunk, 0)


def first_kernel(rows, listed, tiles, degree, *refs):
    gathered, (out, high, low) = refs[:8], refs[8:]
    blocks = gathered[0].shape[0] // TILE
    for i, ref in enumerate(gathered):

        def load(j, _, i=i, ref=ref):
            at = pl.ds(pl.multiple_of(j * TILE, TILE), TILE)
            high[i * blocks + j], low[i * blocks + j] = split(ref[at, :])
            return 0

        lax.fori_loop(0, blocks, load, 0)
    add_products(0, rows, listed, tiles, degree, high, low, out)


def next_kernel(stage, rows, listed, tiles, degree, high, low, out):
    add_products(stage, rows, listed, tiles, degree, high, low, out)


def products(stage, rows, listed, tiles, degree, sources):
    n = PIECES[stage]
    outs = [jax.ShapeDtypeStruct((2 * n, rows, F), F32)]
    if stage == 0:
        kernel = functools.partial(first_kernel, rows)
        outs += [jax.ShapeDtypeStruct((48, TILE, F), BF)] * 2
    else:
        kernel = functools.partial(next_kernel, stage, rows)
    out, *halves = pl.pallas_call(
        kernel,
        out_shape=tuple(outs),
        in_specs=[SMEM] + [VMEM] * (2 + len(sources)),
        out_specs=(VMEM,) * len(outs),
        compiler_params=pltpu.CompilerParams(vmem_limit_bytes=32 << 20),
        cost_estimate=pl.CostEstimate(flops=10**9 * n, bytes_accessed=n * 40 * 10**5, transcendentals=0),
        name=("early", "mid", "late")[stage],
    )(listed, tiles, degree, *sources)
    return out[:n], out[n:], *halves


def gather(state, meanwhile=None):
    a, b, c = (send(state, in_plane(d, 0)) for d in (1, -1, 2))
    a, b, c, meanwhile = lax.optimization_barrier((a, b, c, meanwhile))
    up, down = in_plane(1, 1), in_plane(-1, 1)
    top, low = jnp.concatenate([state, a], axis=0), jnp.concatenate([b, c], axis=0)
    top, low = lax.optimization_barrier((top, low))
    top_up, top_down = send(top, up), send(top, down)
    low_up, low_down = send(low, up), send(low, down)
    return (top, low, top_up, low_up, top_down, low_down, send(top_up, up), send(low_down, down)), meanwhile


def body(features, tiles, tile_col, tile_slot, mirror_list, tile_counts, self_weight, neigh_weight):
    z, c, x, y = (lax.axis_index(a).astype(jnp.int32) for a in AXES)
    place = jnp.stack([z, c, jnp.where(c == 0, x, y), jnp.where(c == 0, y, x)])
    listed = plan(place, tile_col, tile_slot, mirror_list.reshape(-1), tile_counts)
    up, down = along_z(1), along_z(-1)
    state = features
    for layer in range(LAYERS):
        rows = ROWS + 8 if layer == 0 else ROWS
        if layer == 0:
            gathered, listed = gather(state, listed)
            degree_part = degrees(listed, tiles)
        else:
            gathered, _ = gather(state)
        sent, kept, high, low = products(0, rows, listed, tiles, degree_part, gathered)
        got = send(sent, PAIR)
        sent_mid, kept_mid = products(1, rows, listed, tiles, degree_part, (high, low))
        got, sent_mid, high, low = lax.optimization_barrier((got, sent_mid, high, low))
        got_mid = send(sent_mid, PAIR)
        f, g = send(kept[0] + got[0], up), send(kept[1] + got[1], down)
        sent_last, kept_last = products(2, rows, listed, tiles, degree_part, (high, low))
        f, g, got_mid, sent_last = lax.optimization_barrier((f, g, got_mid, sent_last))
        got_last = send(sent_last, PAIR)
        f = send(f + (kept_mid[0] + got_mid[0]), up)
        g = send(g + (kept_mid[1] + got_mid[1]), down)
        f = send(f + (kept_last[0] + got_last[0]), up)
        g = send(g + (kept_last[1] + got_last[1]), down)
        f = send(f + (kept_last[2] + got_last[2]), up)
        total = f + (g + (kept_last[3] + got_last[3]))
        if layer == 0:
            degree = total[ROWS : ROWS + BLK_DEV, :TILE].reshape(ROWS)
            total = total[:ROWS]
        neighbour_mean = (state + total) / (1.0 + degree)[:, None]
        activated = jax.nn.relu(
            jnp.dot(state, self_weight[layer], precision=lax.Precision.HIGHEST)
            + jnp.dot(neighbour_mean, neigh_weight[layer], precision=lax.Precision.HIGHEST)
        )
        state = activated * lax.rsqrt(jnp.mean(activated * activated, axis=1, keepdims=True) + 1e-05)
    return state


def solution(mesh):
    fine = Mesh(mesh.devices.reshape(NZ, NC, NX, NY), AXES)
    placed = (
        P(AXES, None),
        P(AXES, None, None),
        P(AXES),
        P(AXES),
        P(AXES, None, None),
        P(AXES),
        P(),
        P(),
    )
    return jax.shard_map(body, mesh=fine, in_specs=placed, out_specs=P(AXES, None), check_vma=False)
```

profile of v0, /device:TPU:24, one launch (start us, length us, event | category | flops | bytes accessed | tf_op | source)
XLA Modules:
  0.0 200.0 jit_solution(13399899694285214225)
XLA Ops:
  7.7 7.5 %plan.1.listed = s32[656]{0:T(1024)} custom-call(s32[4]{0:T(128)} %pad_add_fusion.place, s32[96]{0:T(128)} %col.1, s32[96]{0:T(128)} %slot.1, s32[32]{0:T(128)} %reshape.43.mirror, s32[1]{0:T(128)S(6)} %copy.17.count), custom_call_target="tpu_custom_call" | custom-call | bytes 20000000 | tf_op jit(solution)/shard_map/plan/pallas_call | solution.py:137
  20.5 7.9 %collective-permute-done.3.refs_2_ = f32[768,256]{1,0:T(8,128)S(1)} collective-permute-done((f32[768,256]{1,0:T(8,128)S(1)}, f32[768,256]{1,0:T(8,128)S(1)}, u32[]{:S(2)}, u32[]{:S(2)}) %collective-permute-start.3) | collective-permute-done | bytes 786464 | tf_op jit(solution)/shard_map/ppermute | solution.py:60
  33.2 4.5 %degrees.1.degree = f32[16,8,128]{2,1,0:T(8,128)S(1)} custom-call(s32[656]{0:T(1024)S(1)} %copy-done.2, f32[96,128,128]{2,1,0:T(8,128)S(1)} %copy-done), custom_call_target="tpu_custom_call" | custom-call | flops 100000000 | bytes 20000000 | tf_op jit(solution)/shard_map/degrees/pallas_call | solution.py:173
  38.2 7.0 %collective-permute-done.7.refs_6_ = f32[768,256]{1,0:T(8,128)S(1)} collective-permute-done((f32[768,256]{1,0:T(8,128)S(1)}, f32[768,256]{1,0:T(8,128)S(1)}, u32[]{:S(2)}, u32[]{:S(2)}) %collective-permute-start.7) | collective-permute-done | bytes 786464 | tf_op jit(solution)/shard_map/ppermute | solution.py:60
  54.7 3.6 %collective-permute-start.11 = (f32[392,256]{1,0:T(8,128)S(1)}, f32[392,256]{1,0:T(8,128)S(1)}, u32[]{:S(2)}, u32[]{:S(2)}) collective-permute-start(f32[392,256]{1,0:T(8,128)S(1)} %get-tuple-element.77), channel_id=1, source_target_pairs={{0,224},{1,225},{2,226},{3,227},{4,228},{5,229},{6,230},{7,231},{8... | collective-permute-start | bytes 1204232 | tf_op jit(solution)/shard_map/ppermute | solution.py:60
  58.3 3.6 %late.2 = f32[8,392,256]{2,1,0:T(8,128)S(1)} custom-call(s32[656]{0:T(1024)S(1)} %copy-done.2, f32[96,128,128]{2,1,0:T(8,128)S(1)} %copy-done.1, f32[16,8,128]{2,1,0:T(8,128)S(1)} %degrees.1.degree, bf16[48,128,256]{2,1,0:T(8,128)(2,1)S(1)} %get-tuple-element.49.high, bf16[48,128,256]{2,1,0:T(8,128)(2,1)S(1)} %get-tuple-element.50.low), custom_call_target="tpu_custom_call" | custom-call | flops 4000000000 | bytes 16000000 | tf_op jit(solution)/shard_map/late/pallas_call | solution.py:239
  62.0 3.8 %collective-permute-done.10 = f32[392,256]{1,0:T(8,128)S(1)} collective-permute-done((f32[392,256]{1,0:T(8,128)S(1)}, f32[392,256]{1,0:T(8,128)S(1)}, u32[]{:S(2)}, u32[]{:S(2)}) %collective-permute-start.10) | collective-permute-done | bytes 401440 | tf_op jit(solution)/shard_map/ppermute | solution.py:60
  68.4 3.2 %collective-permute-start.17 = (f32[392,256]{1,0:T(8,128)S(1)}, f32[392,256]{1,0:T(8,128)S(1)}, u32[]{:S(2)}, u32[]{:S(2)}) collective-permute-start(f32[392,256]{1,0:T(8,128)S(1)} %get-tuple-element.75), channel_id=1, source_target_pairs={{0,224},{1,225},{2,226},{3,227},{4,228},{5,229},{6,230},{7,231},{8... | collective-permute-start | bytes 1204232 | tf_op jit(solution)/shard_map/ppermute | solution.py:60
  71.7 7.9 %collective-permute-done.13 = f32[392,256]{1,0:T(8,128)S(1)} collective-permute-done((f32[392,256]{1,0:T(8,128)S(1)}, f32[392,256]{1,0:T(8,128)S(1)}, u32[]{:S(2)}, u32[]{:S(2)}) %collective-permute-start.13) | collective-permute-done | bytes 401440 | tf_op jit(solution)/shard_map/ppermute | solution.py:60
  80.6 8.8 %collective-permute-done.15 = f32[392,256]{1,0:T(8,128)S(1)} collective-permute-done((f32[392,256]{1,0:T(8,128)S(1)}, f32[392,256]{1,0:T(8,128)S(1)}, u32[]{:S(2)}, u32[]{:S(2)}) %collective-permute-start.15) | collective-permute-done | bytes 401440 | tf_op jit(solution)/shard_map/ppermute | solution.py:60
  89.6 3.2 %collective-permute-start.18 = (f32[392,256]{1,0:T(8,128)S(1)}, f32[392,256]{1,0:T(8,128)S(1)}, u32[]{:S(2)}, u32[]{:S(2)}) collective-permute-start(f32[392,256]{1,0:T(8,128)S(1)} %get-tuple-element.71), channel_id=1, source_target_pairs={{0,224},{1,225},{2,226},{3,227},{4,228},{5,229},{6,230},{7,231},{8... | collective-permute-start | bytes 1204232 | tf_op jit(solution)/shard_map/ppermute | solution.py:60
  93.3 8.5 %collective-permute-done.16 = f32[392,256]{1,0:T(8,128)S(1)} collective-permute-done((f32[392,256]{1,0:T(8,128)S(1)}, f32[392,256]{1,0:T(8,128)S(1)}, u32[]{:S(2)}, u32[]{:S(2)}) %collective-permute-start.16) | collective-permute-done | bytes 401440 | tf_op jit(solution)/shard_map/ppermute | solution.py:60
  107.5 4.3 %collective-permute-done.19 = f32[384,256]{1,0:T(8,128)S(1)} collective-permute-done((f32[384,256]{1,0:T(8,128)S(1)}, f32[384,256]{1,0:T(8,128)S(1)}, u32[]{:S(2)}, u32[]{:S(2)}) %collective-permute-start.19) | collective-permute-done | bytes 393248 | tf_op jit(solution)/shard_map/ppermute | solution.py:60
  111.8 3.8 %collective-permute-done.20 = f32[384,256]{1,0:T(8,128)S(1)} collective-permute-done((f32[384,256]{1,0:T(8,128)S(1)}, f32[384,256]{1,0:T(8,128)S(1)}, u32[]{:S(2)}, u32[]{:S(2)}) %collective-permute-start.20) | collective-permute-done | bytes 393248 | tf_op jit(solution)/shard_map/ppermute | solution.py:60
  121.2 7.9 %collective-permute-done.22.refs_2_ = f32[768,256]{1,0:T(8,128)S(1)} collective-permute-done((f32[768,256]{1,0:T(8,128)S(1)}, f32[768,256]{1,0:T(8,128)S(1)}, u32[]{:S(2)}, u32[]{:S(2)}) %collective-permute-start.22) | collective-permute-done | bytes 786464 | tf_op jit(solution)/shard_map/ppermute | solution.py:60
  131.1 6.4 %collective-permute-done.23.refs_3_ = f32[768,256]{1,0:T(8,128)S(1)} collective-permute-done((f32[768,256]{1,0:T(8,128)S(1)}, f32[768,256]{1,0:T(8,128)S(1)}, u32[]{:S(2)}, u32[]{:S(2)}) %collective-permute-start.23) | collective-permute-done | bytes 786464 | tf_op jit(solution)/shard_map/ppermute | solution.py:60
  139.5 6.5 %collective-permute-done.26.refs_6_ = f32[768,256]{1,0:T(8,128)S(1)} collective-permute-done((f32[768,256]{1,0:T(8,128)S(1)}, f32[768,256]{1,0:T(8,128)S(1)}, u32[]{:S(2)}, u32[]{:S(2)}) %collective-permute-start.26) | collective-permute-done | bytes 786464 | tf_op jit(solution)/shard_map/ppermute | solution.py:60
  154.0 3.2 %collective-permute-start.30 = (f32[384,256]{1,0:T(8,128)S(1)}, f32[384,256]{1,0:T(8,128)S(1)}, u32[]{:S(2)}, u32[]{:S(2)}) collective-permute-start(f32[384,256]{1,0:T(8,128)S(1)} %get-tuple-element.81), channel_id=1, source_target_pairs={{0,224},{1,225},{2,226},{3,227},{4,228},{5,229},{6,230},{7,231},{8... | collective-permute-start | bytes 1179656 | tf_op jit(solution)/shard_map/ppermute | solution.py:60
  157.3 3.6 %late.3 = f32[8,384,256]{2,1,0:T(8,128)S(1)} custom-call(s32[656]{0:T(1024)S(1)} %copy-done.2, f32[96,128,128]{2,1,0:T(8,128)S(1)} %copy-done.1, f32[16,8,128]{2,1,0:T(8,128)S(1)} %degrees.1.degree, bf16[48,128,256]{2,1,0:T(8,128)(2,1)S(1)} %get-tuple-element.65.high, bf16[48,128,256]{2,1,0:T(8,128)(2,1)S(1)} %get-tuple-element.66.low), custom_call_target="tpu_custom_call" | custom-call | flops 4000000000 | bytes 16000000 | tf_op jit(solution)/shard_map/late/pallas_call | solution.py:239
  161.0 6.1 %collective-permute-done.29 = f32[384,256]{1,0:T(8,128)S(1)} collective-permute-done((f32[384,256]{1,0:T(8,128)S(1)}, f32[384,256]{1,0:T(8,128)S(1)}, u32[]{:S(2)}, u32[]{:S(2)}) %collective-permute-start.29) | collective-permute-done | bytes 393248 | tf_op jit(solution)/shard_map/ppermute | solution.py:60
  167.3 3.2 %collective-permute-start.36 = (f32[384,256]{1,0:T(8,128)S(1)}, f32[384,256]{1,0:T(8,128)S(1)}, u32[]{:S(2)}, u32[]{:S(2)}) collective-permute-start(f32[384,256]{1,0:T(8,128)S(1)} %get-tuple-element.79), channel_id=1, source_target_pairs={{0,224},{1,225},{2,226},{3,227},{4,228},{5,229},{6,230},{7,231},{8... | collective-permute-start | bytes 1179656 | tf_op jit(solution)/shard_map/ppermute | solution.py:60
  170.5 9.6 %collective-permute-done.32 = f32[384,256]{1,0:T(8,128)S(1)} collective-permute-done((f32[384,256]{1,0:T(8,128)S(1)}, f32[384,256]{1,0:T(8,128)S(1)}, u32[]{:S(2)}, u32[]{:S(2)}) %collective-permute-start.32) | collective-permute-done | bytes 393248 | tf_op jit(solution)/shard_map/ppermute | solution.py:60
  180.3 9.0 %collective-permute-done.34 = f32[384,256]{1,0:T(8,128)S(1)} collective-permute-done((f32[384,256]{1,0:T(8,128)S(1)}, f32[384,256]{1,0:T(8,128)S(1)}, u32[]{:S(2)}, u32[]{:S(2)}) %collective-permute-start.34) | collective-permute-done | bytes 393248 | tf_op jit(solution)/shard_map/ppermute | solution.py:60
  193.2 5.3 %collective-permute-done.35 = f32[384,256]{1,0:T(8,128)S(1)} collective-permute-done((f32[384,256]{1,0:T(8,128)S(1)}, f32[384,256]{1,0:T(8,128)S(1)}, u32[]{:S(2)}, u32[]{:S(2)}) %collective-permute-start.35) | collective-permute-done | bytes 393248 | tf_op jit(solution)/shard_map/ppermute | solution.py:60
  (102 shorter events, 60.7 us)
Async XLA Ops:
  0.0 15.2 %collective-permute-start = (f32[384,256]{1,0:T(8,128)}, f32[384,256]{1,0:T(8,128)S(1)}, u32[]{:S(2)}, u32[]{:S(2)}) collective-permute-start(f32[384,256]{1,0:T(8,128)} %param.8), channel_id=1, source_target_pairs={{0,4},{1,5},{2,6},{3,7},{4,8},{5,9},{6,10},{7,11},{8,12},{9,13},{1... | collective-permute-start | bytes 1179656 | tf_op jit(solution)/shard_map/ppermute | solution.py:60
  1.5 13.7 %collective-permute-start.1 = (f32[384,256]{1,0:T(8,128)}, f32[384,256]{1,0:T(8,128)S(1)}, u32[]{:S(2)}, u32[]{:S(2)}) collective-permute-start(f32[384,256]{1,0:T(8,128)} %param.8), channel_id=1, source_target_pairs={{0,12},{1,13},{2,14},{3,15},{4,0},{5,1},{6,2},{7,3},{8,4},{9,5},{1... | collective-permute-start | bytes 1179656 | tf_op jit(solution)/shard_map/ppermute | solution.py:60
  16.6 13.2 %collective-permute-start.6 = (f32[768,256]{1,0:T(8,128)S(1)}, f32[768,256]{1,0:T(8,128)S(1)}, u32[]{:S(2)}, u32[]{:S(2)}) collective-permute-start(f32[768,256]{1,0:T(8,128)S(1)} %get-tuple-element.43.refs_1_), channel_id=1, source_target_pairs={{0,3},{1,0},{2,1},{3,2},{4,7},{5,4},{6,5},{7,6},{8,11},{9,8},{10,9... | collective-permute-start | bytes 2359304 | tf_op jit(solution)/shard_map/ppermute | solution.py:60
  18.4 19.3 %collective-permute-start.4 = (f32[768,256]{1,0:T(8,128)S(1)}, f32[768,256]{1,0:T(8,128)S(1)}, u32[]{:S(2)}, u32[]{:S(2)}) collective-permute-start(f32[768,256]{1,0:T(8,128)S(1)} %get-tuple-element.43.refs_1_), channel_id=1, source_target_pairs={{0,1},{1,2},{2,3},{3,0},{4,5},{5,6},{6,7},{7,4},{8,9},{9,10},{10,1... | collective-permute-start | bytes 2359304 | tf_op jit(solution)/shard_map/ppermute | solution.py:60
  19.8 18.4 %collective-permute-start.5 = (f32[768,256]{1,0:T(8,128)S(1)}, f32[768,256]{1,0:T(8,128)S(1)}, u32[]{:S(2)}, u32[]{:S(2)}) collective-permute-start(f32[768,256]{1,0:T(8,128)S(1)} %get-tuple-element.42.refs_0_), channel_id=1, source_target_pairs={{0,3},{1,0},{2,1},{3,2},{4,7},{5,4},{6,5},{7,6},{8,11},{9,8},{10,9... | collective-permute-start | bytes 2359304 | tf_op jit(solution)/shard_map/ppermute | solution.py:60
  28.4 16.9 %collective-permute-start.7 = (f32[768,256]{1,0:T(8,128)S(1)}, f32[768,256]{1,0:T(8,128)S(1)}, u32[]{:S(2)}, u32[]{:S(2)}) collective-permute-start(f32[768,256]{1,0:T(8,128)S(1)} %collective-permute-done.3.refs_2_), channel_id=1, source_target_pairs={{0,1},{1,2},{2,3},{3,0},{4,5},{5,6},{6,7},{7,4},{8,9},{9,10},{10,1... | collective-permute-start | bytes 2359304 | tf_op jit(solution)/shard_map/ppermute | solution.py:60
  29.8 16.8 %collective-permute-start.8 = (f32[768,256]{1,0:T(8,128)S(1)}, f32[768,256]{1,0:T(8,128)S(1)}, u32[]{:S(2)}, u32[]{:S(2)}) collective-permute-start(f32[768,256]{1,0:T(8,128)S(1)} %collective-permute-done.6.refs_5_), channel_id=1, source_target_pairs={{0,3},{1,0},{2,1},{3,2},{4,7},{5,4},{6,5},{7,6},{8,11},{9,8},{10,9... | collective-permute-start | bytes 2359304 | tf_op jit(solution)/shard_map/ppermute | solution.py:60
  51.7 15.7 %collective-permute-start.12 = (f32[2,392,256]{2,1,0:T(8,128)S(1)}, f32[2,392,256]{2,1,0:T(8,128)S(1)}, u32[]{:S(2)}, u32[]{:S(2)}) collective-permute-start(f32[2,392,256]{2,1,0:T(8,128)S(1)} %slice.198), channel_id=1, source_target_pairs={{0,16},{1,17},{2,18},{3,19},{4,20},{5,21},{6,22},{7,23},{8,24},{9,... | collective-permute-start | bytes 2408456 | tf_op jit(solution)/shard_map/ppermute | solution.py:60
  52.7 13.1 %collective-permute-start.10 = (f32[392,256]{1,0:T(8,128)S(1)}, f32[392,256]{1,0:T(8,128)S(1)}, u32[]{:S(2)}, u32[]{:S(2)}) collective-permute-start(f32[392,256]{1,0:T(8,128)S(1)} %get-tuple-element.78), channel_id=1, source_target_pairs={{0,32},{1,33},{2,34},{3,35},{4,36},{5,37},{6,38},{7,39},{8,40},{9,... | collective-permute-start | bytes 1204232 | tf_op jit(solution)/shard_map/ppermute | solution.py:60
  54.7 12.7 %collective-permute-start.11 = (f32[392,256]{1,0:T(8,128)S(1)}, f32[392,256]{1,0:T(8,128)S(1)}, u32[]{:S(2)}, u32[]{:S(2)}) collective-permute-start(f32[392,256]{1,0:T(8,128)S(1)} %get-tuple-element.77), channel_id=1, source_target_pairs={{0,224},{1,225},{2,226},{3,227},{4,228},{5,229},{6,230},{7,231},{8... | collective-permute-start | bytes 1204232 | tf_op jit(solution)/shard_map/ppermute | solution.py:60
  89.5 12.3 %collective-permute-start.16 = (f32[392,256]{1,0:T(8,128)S(1)}, f32[392,256]{1,0:T(8,128)S(1)}, u32[]{:S(2)}, u32[]{:S(2)}) collective-permute-start(f32[392,256]{1,0:T(8,128)S(1)} %get-tuple-element.72), channel_id=1, source_target_pairs={{0,32},{1,33},{2,34},{3,35},{4,36},{5,37},{6,38},{7,39},{8,40},{9,... | collective-permute-start | bytes 1204232 | tf_op jit(solution)/shard_map/ppermute | solution.py:60
  89.6 12.2 %collective-permute-start.18 = (f32[392,256]{1,0:T(8,128)S(1)}, f32[392,256]{1,0:T(8,128)S(1)}, u32[]{:S(2)}, u32[]{:S(2)}) collective-permute-start(f32[392,256]{1,0:T(8,128)S(1)} %get-tuple-element.71), channel_id=1, source_target_pairs={{0,224},{1,225},{2,226},{3,227},{4,228},{5,229},{6,230},{7,231},{8... | collective-permute-start | bytes 1204232 | tf_op jit(solution)/shard_map/ppermute | solution.py:60
  103.4 12.2 %collective-permute-start.20 = (f32[384,256]{1,0:T(8,128)S(1)}, f32[384,256]{1,0:T(8,128)S(1)}, u32[]{:S(2)}, u32[]{:S(2)}) collective-permute-start(f32[384,256]{1,0:T(8,128)S(1)} %broadcast_multiply_fusion.1), channel_id=1, source_target_pairs={{0,12},{1,13},{2,14},{3,15},{4,0},{5,1},{6,2},{7,3},{8,4},{9,5},{1... | collective-permute-start | bytes 1179656 | tf_op jit(solution)/shard_map/ppermute | solution.py:60
  117.8 13.2 %collective-permute-start.25 = (f32[768,256]{1,0:T(8,128)S(1)}, f32[768,256]{1,0:T(8,128)S(1)}, u32[]{:S(2)}, u32[]{:S(2)}) collective-permute-start(f32[768,256]{1,0:T(8,128)S(1)} %pad_maximum_fusion.3.refs_1_), channel_id=1, source_target_pairs={{0,3},{1,0},{2,1},{3,2},{4,7},{5,4},{6,5},{7,6},{8,11},{9,8},{10,9... | collective-permute-start | bytes 2359304 | tf_op jit(solution)/shard_map/ppermute | solution.py:60
  119.1 18.4 %collective-permute-start.23 = (f32[768,256]{1,0:T(8,128)S(1)}, f32[768,256]{1,0:T(8,128)S(1)}, u32[]{:S(2)}, u32[]{:S(2)}) collective-permute-start(f32[768,256]{1,0:T(8,128)S(1)} %pad_maximum_fusion.3.refs_1_), channel_id=1, source_target_pairs={{0,1},{1,2},{2,3},{3,0},{4,5},{5,6},{6,7},{7,4},{8,9},{9,10},{10,1... | collective-permute-start | bytes 2359304 | tf_op jit(solution)/shard_map/ppermute | solution.py:60
  121.1 18.4 %collective-permute-start.24 = (f32[768,256]{1,0:T(8,128)S(1)}, f32[768,256]{1,0:T(8,128)S(1)}, u32[]{:S(2)}, u32[]{:S(2)}) collective-permute-start(f32[768,256]{1,0:T(8,128)S(1)} %pad_maximum_fusion.2.refs_0_), channel_id=1, source_target_pairs={{0,3},{1,0},{2,1},{3,2},{4,7},{5,4},{6,5},{7,6},{8,11},{9,8},{10,9... | collective-permute-start | bytes 2359304 | tf_op jit(solution)/shard_map/ppermute | solution.py:60
  129.1 16.9 %collective-permute-start.26 = (f32[768,256]{1,0:T(8,128)S(1)}, f32[768,256]{1,0:T(8,128)S(1)}, u32[]{:S(2)}, u32[]{:S(2)}) collective-permute-start(f32[768,256]{1,0:T(8,128)S(1)} %collective-permute-done.22.refs_2_), channel_id=1, source_target_pairs={{0,1},{1,2},{2,3},{3,0},{4,5},{5,6},{6,7},{7,4},{8,9},{9,10},{10,1... | collective-permute-start | bytes 2359304 | tf_op jit(solution)/shard_map/ppermute | solution.py:60
  131.1 16.8 %collective-permute-start.27 = (f32[768,256]{1,0:T(8,128)S(1)}, f32[768,256]{1,0:T(8,128)S(1)}, u32[]{:S(2)}, u32[]{:S(2)}) collective-permute-start(f32[768,256]{1,0:T(8,128)S(1)} %collective-permute-done.25.refs_5_), channel_id=1, source_target_pairs={{0,3},{1,0},{2,1},{3,2},{4,7},{5,4},{6,5},{7,6},{8,11},{9,8},{10,9... | collective-permute-start | bytes 2359304 | tf_op jit(solution)/shard_map/ppermute | solution.py:60
  152.9 14.1 %collective-permute-start.31 = (f32[2,384,256]{2,1,0:T(8,128)S(1)}, f32[2,384,256]{2,1,0:T(8,128)S(1)}, u32[]{:S(2)}, u32[]{:S(2)}) collective-permute-start(f32[2,384,256]{2,1,0:T(8,128)S(1)} %slice.212), channel_id=1, source_target_pairs={{0,16},{1,17},{2,18},{3,19},{4,20},{5,21},{6,22},{7,23},{8,24},{9,... | collective-permute-start | bytes 2359304 | tf_op jit(solution)/shard_map/ppermute | solution.py:60
  154.0 13.1 %collective-permute-start.29 = (f32[384,256]{1,0:T(8,128)S(1)}, f32[384,256]{1,0:T(8,128)S(1)}, u32[]{:S(2)}, u32[]{:S(2)}) collective-permute-start(f32[384,256]{1,0:T(8,128)S(1)} %get-tuple-element.82), channel_id=1, source_target_pairs={{0,32},{1,33},{2,34},{3,35},{4,36},{5,37},{6,38},{7,39},{8,40},{9,... | collective-permute-start | bytes 1179656 | tf_op jit(solution)/shard_map/ppermute | solution.py:60
  154.0 13.0 %collective-permute-start.30 = (f32[384,256]{1,0:T(8,128)S(1)}, f32[384,256]{1,0:T(8,128)S(1)}, u32[]{:S(2)}, u32[]{:S(2)}) collective-permute-start(f32[384,256]{1,0:T(8,128)S(1)} %get-tuple-element.81), channel_id=1, source_target_pairs={{0,224},{1,225},{2,226},{3,227},{4,228},{5,229},{6,230},{7,231},{8... | collective-permute-start | bytes 1179656 | tf_op jit(solution)/shard_map/ppermute | solution.py:60
  167.1 13.1 %collective-permute-start.33 = (f32[4,384,256]{2,1,0:T(8,128)S(1)}, f32[4,384,256]{2,1,0:T(8,128)S(1)}, u32[]{:S(2)}, u32[]{:S(2)}) collective-permute-start(f32[4,384,256]{2,1,0:T(8,128)S(1)} %slice.213), channel_id=1, source_target_pairs={{0,16},{1,17},{2,18},{3,19},{4,20},{5,21},{6,22},{7,23},{8,24},{9,... | collective-permute-start | bytes 4718600 | tf_op jit(solution)/shard_map/ppermute | solution.py:60
  167.2 12.9 %collective-permute-start.32 = (f32[384,256]{1,0:T(8,128)S(1)}, f32[384,256]{1,0:T(8,128)S(1)}, u32[]{:S(2)}, u32[]{:S(2)}) collective-permute-start(f32[384,256]{1,0:T(8,128)S(1)} %get-tuple-element.80), channel_id=1, source_target_pairs={{0,32},{1,33},{2,34},{3,35},{4,36},{5,37},{6,38},{7,39},{8,40},{9,... | collective-permute-start | bytes 1179656 | tf_op jit(solution)/shard_map/ppermute | solution.py:60
  167.3 13.0 %collective-permute-start.36 = (f32[384,256]{1,0:T(8,128)S(1)}, f32[384,256]{1,0:T(8,128)S(1)}, u32[]{:S(2)}, u32[]{:S(2)}) collective-permute-start(f32[384,256]{1,0:T(8,128)S(1)} %get-tuple-element.79), channel_id=1, source_target_pairs={{0,224},{1,225},{2,226},{3,227},{4,228},{5,229},{6,230},{7,231},{8... | collective-permute-start | bytes 1179656 | tf_op jit(solution)/shard_map/ppermute | solution.py:60
  (20 other events, 203.4 us)
where the time goes:
time: 203 us; the launch traced here: 200 us
  waiting for transfers between devices  113 us (56%)
  starting transfers between devices  47.2 us (23%)
  Pallas kernels  27.6 us (14%)
  local copies, waits for them, and re-layouts  4.58 us (2%)
  other arithmetic  4.05 us (2%)
  matrix products  2.21 us (1%)
    ppermute x38, waiting for transfers between devices, send(): return lax.ppermute(value, AXES, pairs)  113 us
    ppermute x38, starting transfers between devices, send(): return lax.ppermute(value, AXES, pairs)  47.2 us
    pallas_call x6, Pallas kernels, products(): pl.pallas_call(kernel, out_shape=tuple(outs), in_specs=[SMEM] + [VMEM] *...  15.6 us
    pallas_call x1, Pallas kernels, plan(): pl.pallas_call(plan_kernel, out_shape=jax.ShapeDtypeStruct((LISTED,), jnp...  7.47 us
    pallas_call x1, Pallas kernels, degrees(): pl.pallas_call(degree_kernel, out_shape=jax.ShapeDtypeStruct((2 * NZ, 8,...  4.51 us
  transfers between devices with their start and end apart: 38, of which 24 were waited for; matrix products, arithmetic and copies ran while one was open for 2% of the time, Pallas kernels for 11%

commit v1 on v0

--- a/solution.py
+++ b/solution.py
@@ -17,8 +17,8 @@
 NZ, NC, NX, NY = 8, 2, 4, 4
 AXES = ("z", "c", "x", "y")
 UNROLL = 8
-PIECES = (2, 2, 4)
-BASE = (0, 4, 8)
+PIECES = (1, 2, 5)
+BASE = (0, 2, 6)
 SEGMENTS = len(PIECES)
 SLOTS = 2 * TILES_DEV + SEGMENTS * UNROLL
 SOURCE, DEST, BOUNDS = SLOTS, 2 * SLOTS, 3 * SLOTS
@@ -71,7 +71,7 @@
 
 def piece_of(r):
     return jnp.where(
-        r == 3, 0, jnp.where(r == 6, 1, jnp.where(r == 2, 0, jnp.where(r == 7, 1, jnp.where(r == 1, 2, 3))))
+        (r == 5) | (r == 6), 1, jnp.where(r == 1, 2, jnp.where(r == 7, 3, jnp.where(r == 0, 4, 0)))
     )
 
 
@@ -85,11 +85,10 @@
         g = sl // CAP
         gz, gc = g // NC, g % NC
         r = lax.bitwise_and(jnp.where(gc == 0, gz - z, z - gz) + NZ, NZ - 1)
-        first = jnp.logical_or(r == 4, r == 5)
-        second = jnp.logical_or(r == 3, r == 6)
-        seg = jnp.where(first, 0, jnp.where(second, 1, 2))
-        piece = jnp.where(first, r - 4, piece_of(r)) + BASE[1] * seg
-        piece += jnp.where(gc == c, jnp.where(seg == 2, PIECES[2], PIECES[0]), 0)
+        seg = jnp.where(r == 4, 0, jnp.where((r == 3) | (r == 5), 1, 2))
+        piece = piece_of(r) + jnp.where(seg == 0, BASE[0], jnp.where(seg == 1, BASE[1], BASE[2]))
+        kept = jnp.where(seg == 0, PIECES[0], jnp.where(seg == 1, PIECES[1], PIECES[2]))
+        piece += jnp.where(gc == c, kept, 0)
         seg = jnp.where(t < count[0], seg, SEGMENTS)
         cls[t] = seg * 64 + piece * 4 + mirror[sl]
         nxt[seg] = nxt[seg] + 1
@@ -277,16 +276,16 @@
         sent_mid, kept_mid = products(1, rows, listed, tiles, degree_part, (high, low))
         got, sent_mid, high, low = lax.optimization_barrier((got, sent_mid, high, low))
         got_mid = send(sent_mid, PAIR)
-        f, g = send(kept[0] + got[0], up), send(kept[1] + got[1], down)
+        f = send(kept[0] + got[0], up)
         sent_last, kept_last = products(2, rows, listed, tiles, degree_part, (high, low))
-        f, g, got_mid, sent_last = lax.optimization_barrier((f, g, got_mid, sent_last))
+        f, got_mid, sent_last = lax.optimization_barrier((f, got_mid, sent_last))
         got_last = send(sent_last, PAIR)
-        f = send(f + (kept_mid[0] + got_mid[0]), up)
-        g = send(g + (kept_mid[1] + got_mid[1]), down)
-        f = send(f + (kept_last[0] + got_last[0]), up)
-        g = send(g + (kept_last[1] + got_last[1]), down)
-        f = send(f + (kept_last[2] + got_last[2]), up)
-        total = f + (g + (kept_last[3] + got_last[3]))
+        f, g = f + (kept_mid[0] + got_mid[0]), kept_mid[1] + got_mid[1]
+        f, g = send(f, up), send(g, down)
+        p = lax.optimization_barrier(tuple(kept_last[i] + got_last[i] for i in range(5)))
+        f, g = send(f + p[0], up), send(g + p[1], down)
+        f, g = send(f + p[2], up), send(g + p[3], down)
+        total = f + (g + p[4])
         if layer == 0:
             degree = total[ROWS : ROWS + BLK_DEV, :TILE].reshape(ROWS)
             total = total[:ROWS]

time: 203 us -> 200 us (0.985); the launches traced: 200 us -> 199 us
  starting transfers between devices: 47.2 us -> 49.6 us
    ppermute x38, starting transfers between devices: 47.2 us -> 49.6 us  [send(): return lax.ppermute(value, AXES, pairs)]
    ppermute x38, waiting for transfers between devices: 113 us -> 111 us  [send(): return lax.ppermute(value, AXES, pairs)]
  transfers between devices with their start and end apart: 38 -> 38, of which waited for: 24 -> 20; matrix products, arithmetic and copies ran while one was open for 2% -> 2% of each run, Pallas kernels for 11% -> 11%
where the time goes in v1:
time: 200 us; the launch traced here: 199 us
  waiting for transfers between devices  111 us (56%)
  starting transfers between devices  49.6 us (25%)
  Pallas kernels  26.3 us (13%)
  local copies, waits for them, and re-layouts  4.68 us (2%)
  other arithmetic  4.18 us (2%)
  matrix products  2.2 us (1%)
    ppermute x38, waiting for transfers between devices, send(): return lax.ppermute(value, AXES, pairs)  111 us
    ppermute x38, starting transfers between devices, send(): return lax.ppermute(value, AXES, pairs)  49.6 us
    pallas_call x6, Pallas kernels, products(): pl.pallas_call(kernel, out_shape=tuple(outs), in_specs=[SMEM] + [VMEM] *...  14.7 us
    pallas_call x1, Pallas kernels, plan(): pl.pallas_call(plan_kernel, out_shape=jax.ShapeDtypeStruct((LISTED,), jnp...  7.48 us
    pallas_call x1, Pallas kernels, degrees(): pl.pallas_call(degree_kernel, out_shape=jax.ShapeDtypeStruct((2 * NZ, 8,...  4.11 us
  transfers between devices with their start and end apart: 38, of which 20 were waited for; matrix products, arithmetic and copies ran while one was open for 2% of the time, Pallas kernels for 11%

profile of v1, /device:TPU:24, one launch (start us, length us, event | category | flops | bytes accessed | tf_op | source)
XLA Modules:
  0.0 199.3 jit_solution(4441965983579149117)
XLA Ops:
  7.6 7.5 %plan.1.listed = s32[656]{0:T(1024)} custom-call(s32[4]{0:T(128)} %pad_add_fusion.place, s32[96]{0:T(128)} %col.1, s32[96]{0:T(128)} %slot.1, s32[32]{0:T(128)} %reshape.43.mirror, s32[1]{0:T(128)S(6)} %copy.17.count), custom_call_target="tpu_custom_call" | custom-call | bytes 20000000 | tf_op jit(solution)/shard_map/plan/pallas_call | solution.py:136
  21.6 6.7 %collective-permute-done.3.refs_2_ = f32[768,256]{1,0:T(8,128)S(1)} collective-permute-done((f32[768,256]{1,0:T(8,128)S(1)}, f32[768,256]{1,0:T(8,128)S(1)}, u32[]{:S(2)}, u32[]{:S(2)}) %collective-permute-start.3) | collective-permute-done | bytes 786464 | tf_op jit(solution)/shard_map/ppermute | solution.py:60
  33.2 4.1 %degrees.1.degree = f32[16,8,128]{2,1,0:T(8,128)S(1)} custom-call(s32[656]{0:T(1024)S(1)} %copy-done.2, f32[96,128,128]{2,1,0:T(8,128)S(1)} %copy-done), custom_call_target="tpu_custom_call" | custom-call | flops 100000000 | bytes 20000000 | tf_op jit(solution)/shard_map/degrees/pallas_call | solution.py:172
  38.5 6.7 %collective-permute-done.7.refs_6_ = f32[768,256]{1,0:T(8,128)S(1)} collective-permute-done((f32[768,256]{1,0:T(8,128)S(1)}, f32[768,256]{1,0:T(8,128)S(1)}, u32[]{:S(2)}, u32[]{:S(2)}) %collective-permute-start.7) | collective-permute-done | bytes 786464 | tf_op jit(solution)/shard_map/ppermute | solution.py:60
  54.1 3.7 %late.2 = f32[10,392,256]{2,1,0:T(8,128)S(1)} custom-call(s32[656]{0:T(1024)S(1)} %copy-done.2, f32[96,128,128]{2,1,0:T(8,128)S(1)} %copy-done.1, f32[16,8,128]{2,1,0:T(8,128)S(1)} %degrees.1.degree, bf16[48,128,256]{2,1,0:T(8,128)(2,1)S(1)} %get-tuple-element.57.high, bf16[48,128,256]{2,1,0:T(8,128)(2,1)S(1)} %get-tuple-element.58.low), custom_call_target="tpu_custom_call" | custom-call | flops 5000000000 | bytes 20000000 | tf_op jit(solution)/shard_map/late/pallas_call | solution.py:238
  57.9 5.2 %collective-permute-done.10 = f32[392,256]{1,0:T(8,128)S(1)} collective-permute-done((f32[392,256]{1,0:T(8,128)S(1)}, f32[392,256]{1,0:T(8,128)S(1)}, u32[]{:S(2)}, u32[]{:S(2)}) %collective-permute-start.10) | collective-permute-done | bytes 401440 | tf_op jit(solution)/shard_map/ppermute | solution.py:60
  63.5 3.3 %collective-permute-start.16 = (f32[392,256]{1,0:T(8,128)S(1)}, f32[392,256]{1,0:T(8,128)S(1)}, u32[]{:S(2)}, u32[]{:S(2)}) collective-permute-start(f32[392,256]{1,0:T(8,128)S(1)} %fusion.2), channel_id=1, source_target_pairs={{0,224},{1,225},{2,226},{3,227},{4,228},{5,229},{6,230},{7,231},{8... | collective-permute-start | bytes 1204232 | tf_op jit(solution)/shard_map/ppermute | solution.py:60
  67.3 8.0 %collective-permute-done.12 = f32[392,256]{1,0:T(8,128)S(1)} collective-permute-done((f32[392,256]{1,0:T(8,128)S(1)}, f32[392,256]{1,0:T(8,128)S(1)}, u32[]{:S(2)}, u32[]{:S(2)}) %collective-permute-start.12) | collective-permute-done | bytes 401440 | tf_op jit(solution)/shard_map/ppermute | solution.py:60
  75.5 3.3 %collective-permute-start.17 = (f32[392,256]{1,0:T(8,128)S(1)}, f32[392,256]{1,0:T(8,128)S(1)}, u32[]{:S(2)}, u32[]{:S(2)}) collective-permute-start(f32[392,256]{1,0:T(8,128)S(1)} %add.196), channel_id=1, source_target_pairs={{0,224},{1,225},{2,226},{3,227},{4,228},{5,229},{6,230},{7,231},{8... | collective-permute-start | bytes 1204232 | tf_op jit(solution)/shard_map/ppermute | solution.py:60
  78.8 9.7 %collective-permute-done.14 = f32[392,256]{1,0:T(8,128)S(1)} collective-permute-done((f32[392,256]{1,0:T(8,128)S(1)}, f32[392,256]{1,0:T(8,128)S(1)}, u32[]{:S(2)}, u32[]{:S(2)}) %collective-permute-start.14) | collective-permute-done | bytes 401440 | tf_op jit(solution)/shard_map/ppermute | solution.py:60
  88.8 3.3 %collective-permute-start.18 = (f32[392,256]{1,0:T(8,128)S(1)}, f32[392,256]{1,0:T(8,128)S(1)}, u32[]{:S(2)}, u32[]{:S(2)}) collective-permute-start(f32[392,256]{1,0:T(8,128)S(1)} %add.197), channel_id=1, source_target_pairs={{0,224},{1,225},{2,226},{3,227},{4,228},{5,229},{6,230},{7,231},{8... | collective-permute-start | bytes 1204232 | tf_op jit(solution)/shard_map/ppermute | solution.py:60
  92.6 8.6 %collective-permute-done.15 = f32[392,256]{1,0:T(8,128)S(1)} collective-permute-done((f32[392,256]{1,0:T(8,128)S(1)}, f32[392,256]{1,0:T(8,128)S(1)}, u32[]{:S(2)}, u32[]{:S(2)}) %collective-permute-start.15) | collective-permute-done | bytes 401440 | tf_op jit(solution)/shard_map/ppermute | solution.py:60
  106.6 5.0 %collective-permute-done.21 = f32[384,256]{1,0:T(8,128)S(1)} collective-permute-done((f32[384,256]{1,0:T(8,128)S(1)}, f32[384,256]{1,0:T(8,128)S(1)}, u32[]{:S(2)}, u32[]{:S(2)}) %collective-permute-start.21) | collective-permute-done | bytes 393248 | tf_op jit(solution)/shard_map/ppermute | solution.py:60
  111.5 4.2 %collective-permute-done.20 = f32[384,256]{1,0:T(8,128)S(1)} collective-permute-done((f32[384,256]{1,0:T(8,128)S(1)}, f32[384,256]{1,0:T(8,128)S(1)}, u32[]{:S(2)}, u32[]{:S(2)}) %collective-permute-start.20) | collective-permute-done | bytes 393248 | tf_op jit(solution)/shard_map/ppermute | solution.py:60
  121.2 6.7 %collective-permute-done.22.refs_2_ = f32[768,256]{1,0:T(8,128)S(1)} collective-permute-done((f32[768,256]{1,0:T(8,128)S(1)}, f32[768,256]{1,0:T(8,128)S(1)}, u32[]{:S(2)}, u32[]{:S(2)}) %collective-permute-start.22) | collective-permute-done | bytes 786464 | tf_op jit(solution)/shard_map/ppermute | solution.py:60
  130.3 8.4 %collective-permute-done.24.refs_4_ = f32[768,256]{1,0:T(8,128)S(1)} collective-permute-done((f32[768,256]{1,0:T(8,128)S(1)}, f32[768,256]{1,0:T(8,128)S(1)}, u32[]{:S(2)}, u32[]{:S(2)}) %collective-permute-start.24) | collective-permute-done | bytes 786464 | tf_op jit(solution)/shard_map/ppermute | solution.py:60
  138.8 6.1 %collective-permute-done.26.refs_6_ = f32[768,256]{1,0:T(8,128)S(1)} collective-permute-done((f32[768,256]{1,0:T(8,128)S(1)}, f32[768,256]{1,0:T(8,128)S(1)}, u32[]{:S(2)}, u32[]{:S(2)}) %collective-permute-start.26) | collective-permute-done | bytes 786464 | tf_op jit(solution)/shard_map/ppermute | solution.py:60
  152.3 3.6 %late.3 = f32[10,384,256]{2,1,0:T(8,128)S(1)} custom-call(s32[656]{0:T(1024)S(1)} %copy-done.2, f32[96,128,128]{2,1,0:T(8,128)S(1)} %copy-done.1, f32[16,8,128]{2,1,0:T(8,128)S(1)} %degrees.1.degree, bf16[48,128,256]{2,1,0:T(8,128)(2,1)S(1)} %get-tuple-element.77.high, bf16[48,128,256]{2,1,0:T(8,128)(2,1)S(1)} %get-tuple-element.78.low), custom_call_target="tpu_custom_call" | custom-call | flops 5000000000 | bytes 20000000 | tf_op jit(solution)/shard_map/late/pallas_call | solution.py:238
  156.1 5.1 %collective-permute-done.29 = f32[384,256]{1,0:T(8,128)S(1)} collective-permute-done((f32[384,256]{1,0:T(8,128)S(1)}, f32[384,256]{1,0:T(8,128)S(1)}, u32[]{:S(2)}, u32[]{:S(2)}) %collective-permute-start.29) | collective-permute-done | bytes 393248 | tf_op jit(solution)/shard_map/ppermute | solution.py:60
  161.5 3.3 %collective-permute-start.35 = (f32[384,256]{1,0:T(8,128)S(1)}, f32[384,256]{1,0:T(8,128)S(1)}, u32[]{:S(2)}, u32[]{:S(2)}) collective-permute-start(f32[384,256]{1,0:T(8,128)S(1)} %fusion.10), channel_id=1, source_target_pairs={{0,224},{1,225},{2,226},{3,227},{4,228},{5,229},{6,230},{7,231},{8... | collective-permute-start | bytes 1179656 | tf_op jit(solution)/shard_map/ppermute | solution.py:60
  165.5 8.8 %collective-permute-done.31 = f32[384,256]{1,0:T(8,128)S(1)} collective-permute-done((f32[384,256]{1,0:T(8,128)S(1)}, f32[384,256]{1,0:T(8,128)S(1)}, u32[]{:S(2)}, u32[]{:S(2)}) %collective-permute-start.31) | collective-permute-done | bytes 393248 | tf_op jit(solution)/shard_map/ppermute | solution.py:60
  174.5 3.3 %collective-permute-start.36 = (f32[384,256]{1,0:T(8,128)S(1)}, f32[384,256]{1,0:T(8,128)S(1)}, u32[]{:S(2)}, u32[]{:S(2)}) collective-permute-start(f32[384,256]{1,0:T(8,128)S(1)} %add.224), channel_id=1, source_target_pairs={{0,224},{1,225},{2,226},{3,227},{4,228},{5,229},{6,230},{7,231},{8... | collective-permute-start | bytes 1179656 | tf_op jit(solution)/shard_map/ppermute | solution.py:60
  177.8 8.7 %collective-permute-done.33 = f32[384,256]{1,0:T(8,128)S(1)} collective-permute-done((f32[384,256]{1,0:T(8,128)S(1)}, f32[384,256]{1,0:T(8,128)S(1)}, u32[]{:S(2)}, u32[]{:S(2)}) %collective-permute-start.33) | collective-permute-done | bytes 393248 | tf_op jit(solution)/shard_map/ppermute | solution.py:60
  190.4 7.3 %collective-permute-done.34 = f32[384,256]{1,0:T(8,128)S(1)} collective-permute-done((f32[384,256]{1,0:T(8,128)S(1)}, f32[384,256]{1,0:T(8,128)S(1)}, u32[]{:S(2)}, u32[]{:S(2)}) %collective-permute-start.34) | collective-permute-done | bytes 393248 | tf_op jit(solution)/shard_map/ppermute | solution.py:60
  (110 shorter events, 57.7 us)
Async XLA Ops:
  0.0 15.1 %collective-permute-start.2 = (f32[384,256]{1,0:T(8,128)}, f32[384,256]{1,0:T(8,128)S(1)}, u32[]{:S(2)}, u32[]{:S(2)}) collective-permute-start(f32[384,256]{1,0:T(8,128)} %param.8), channel_id=1, source_target_pairs={{0,8},{1,9},{2,10},{3,11},{4,12},{5,13},{6,14},{7,15},{8,0},{9,1},... | collective-permute-start | bytes 1179656 | tf_op jit(solution)/shard_map/ppermute | solution.py:60
  3.0 12.1 %collective-permute-start.1 = (f32[384,256]{1,0:T(8,128)}, f32[384,256]{1,0:T(8,128)S(1)}, u32[]{:S(2)}, u32[]{:S(2)}) collective-permute-start(f32[384,256]{1,0:T(8,128)} %param.8), channel_id=1, source_target_pairs={{0,12},{1,13},{2,14},{3,15},{4,0},{5,1},{6,2},{7,3},{8,4},{9,5},{1... | collective-permute-start | bytes 1179656 | tf_op jit(solution)/shard_map/ppermute | solution.py:60
  16.3 12.1 %collective-permute-start.3 = (f32[768,256]{1,0:T(8,128)S(1)}, f32[768,256]{1,0:T(8,128)S(1)}, u32[]{:S(2)}, u32[]{:S(2)}) collective-permute-start(f32[768,256]{1,0:T(8,128)S(1)} %get-tuple-element.50.refs_0_), channel_id=1, source_target_pairs={{0,1},{1,2},{2,3},{3,0},{4,5},{5,6},{6,7},{7,4},{8,9},{9,10},{10,1... | collective-permute-start | bytes 2359304 | tf_op jit(solution)/shard_map/ppermute | solution.py:60
  16.8 13.2 %collective-permute-start.6 = (f32[768,256]{1,0:T(8,128)S(1)}, f32[768,256]{1,0:T(8,128)S(1)}, u32[]{:S(2)}, u32[]{:S(2)}) collective-permute-start(f32[768,256]{1,0:T(8,128)S(1)} %get-tuple-element.51.refs_1_), channel_id=1, source_target_pairs={{0,3},{1,0},{2,1},{3,2},{4,7},{5,4},{6,5},{7,6},{8,11},{9,8},{10,9... | collective-permute-start | bytes 2359304 | tf_op jit(solution)/shard_map/ppermute | solution.py:60
  18.4 20.1 %collective-permute-start.5 = (f32[768,256]{1,0:T(8,128)S(1)}, f32[768,256]{1,0:T(8,128)S(1)}, u32[]{:S(2)}, u32[]{:S(2)}) collective-permute-start(f32[768,256]{1,0:T(8,128)S(1)} %get-tuple-element.50.refs_0_), channel_id=1, source_target_pairs={{0,3},{1,0},{2,1},{3,2},{4,7},{5,4},{6,5},{7,6},{8,11},{9,8},{10,9... | collective-permute-start | bytes 2359304 | tf_op jit(solution)/shard_map/ppermute | solution.py:60
  19.2 19.3 %collective-permute-start.4 = (f32[768,256]{1,0:T(8,128)S(1)}, f32[768,256]{1,0:T(8,128)S(1)}, u32[]{:S(2)}, u32[]{:S(2)}) collective-permute-start(f32[768,256]{1,0:T(8,128)S(1)} %get-tuple-element.51.refs_1_), channel_id=1, source_target_pairs={{0,1},{1,2},{2,3},{3,0},{4,5},{5,6},{6,7},{7,4},{8,9},{9,10},{10,1... | collective-permute-start | bytes 2359304 | tf_op jit(solution)/shard_map/ppermute | solution.py:60
  28.4 16.9 %collective-permute-start.7 = (f32[768,256]{1,0:T(8,128)S(1)}, f32[768,256]{1,0:T(8,128)S(1)}, u32[]{:S(2)}, u32[]{:S(2)}) collective-permute-start(f32[768,256]{1,0:T(8,128)S(1)} %collective-permute-done.3.refs_2_), channel_id=1, source_target_pairs={{0,1},{1,2},{2,3},{3,0},{4,5},{5,6},{6,7},{7,4},{8,9},{9,10},{10,1... | collective-permute-start | bytes 2359304 | tf_op jit(solution)/shard_map/ppermute | solution.py:60
  30.0 16.8 %collective-permute-start.8 = (f32[768,256]{1,0:T(8,128)S(1)}, f32[768,256]{1,0:T(8,128)S(1)}, u32[]{:S(2)}, u32[]{:S(2)}) collective-permute-start(f32[768,256]{1,0:T(8,128)S(1)} %collective-permute-done.6.refs_5_), channel_id=1, source_target_pairs={{0,3},{1,0},{2,1},{3,2},{4,7},{5,4},{6,5},{7,6},{8,11},{9,8},{10,9... | collective-permute-start | bytes 2359304 | tf_op jit(solution)/shard_map/ppermute | solution.py:60
  50.8 12.2 %collective-permute-start.11 = (f32[2,392,256]{2,1,0:T(8,128)S(1)}, f32[2,392,256]{2,1,0:T(8,128)S(1)}, u32[]{:S(2)}, u32[]{:S(2)}) collective-permute-start(f32[2,392,256]{2,1,0:T(8,128)S(1)} %slice.186), channel_id=1, source_target_pairs={{0,16},{1,17},{2,18},{3,19},{4,20},{5,21},{6,22},{7,23},{8,24},{9,... | collective-permute-start | bytes 2408456 | tf_op jit(solution)/shard_map/ppermute | solution.py:60
  63.1 12.2 %collective-permute-start.12 = (f32[392,256]{1,0:T(8,128)S(1)}, f32[392,256]{1,0:T(8,128)S(1)}, u32[]{:S(2)}, u32[]{:S(2)}) collective-permute-start(f32[392,256]{1,0:T(8,128)S(1)} %fusion.9), channel_id=1, source_target_pairs={{0,32},{1,33},{2,34},{3,35},{4,36},{5,37},{6,38},{7,39},{8,40},{9,... | collective-permute-start | bytes 1204232 | tf_op jit(solution)/shard_map/ppermute | solution.py:60
  75.4 13.2 %collective-permute-start.14 = (f32[392,256]{1,0:T(8,128)S(1)}, f32[392,256]{1,0:T(8,128)S(1)}, u32[]{:S(2)}, u32[]{:S(2)}) collective-permute-start(f32[392,256]{1,0:T(8,128)S(1)} %add.192), channel_id=1, source_target_pairs={{0,32},{1,33},{2,34},{3,35},{4,36},{5,37},{6,38},{7,39},{8,40},{9,... | collective-permute-start | bytes 1204232 | tf_op jit(solution)/shard_map/ppermute | solution.py:60
  75.5 13.2 %collective-permute-start.17 = (f32[392,256]{1,0:T(8,128)S(1)}, f32[392,256]{1,0:T(8,128)S(1)}, u32[]{:S(2)}, u32[]{:S(2)}) collective-permute-start(f32[392,256]{1,0:T(8,128)S(1)} %add.196), channel_id=1, source_target_pairs={{0,224},{1,225},{2,226},{3,227},{4,228},{5,229},{6,230},{7,231},{8... | collective-permute-start | bytes 1204232 | tf_op jit(solution)/shard_map/ppermute | solution.py:60
  88.6 12.6 %collective-permute-start.15 = (f32[392,256]{1,0:T(8,128)S(1)}, f32[392,256]{1,0:T(8,128)S(1)}, u32[]{:S(2)}, u32[]{:S(2)}) collective-permute-start(f32[392,256]{1,0:T(8,128)S(1)} %add.193), channel_id=1, source_target_pairs={{0,32},{1,33},{2,34},{3,35},{4,36},{5,37},{6,38},{7,39},{8,40},{9,... | collective-permute-start | bytes 1204232 | tf_op jit(solution)/shard_map/ppermute | solution.py:60
  88.8 12.4 %collective-permute-start.18 = (f32[392,256]{1,0:T(8,128)S(1)}, f32[392,256]{1,0:T(8,128)S(1)}, u32[]{:S(2)}, u32[]{:S(2)}) collective-permute-start(f32[392,256]{1,0:T(8,128)S(1)} %add.197), channel_id=1, source_target_pairs={{0,224},{1,225},{2,226},{3,227},{4,228},{5,229},{6,230},{7,231},{8... | collective-permute-start | bytes 1204232 | tf_op jit(solution)/shard_map/ppermute | solution.py:60
  115.9 12.1 %collective-permute-start.22 = (f32[768,256]{1,0:T(8,128)S(1)}, f32[768,256]{1,0:T(8,128)S(1)}, u32[]{:S(2)}, u32[]{:S(2)}) collective-permute-start(f32[768,256]{1,0:T(8,128)S(1)} %pad_maximum_fusion.2.refs_0_), channel_id=1, source_target_pairs={{0,1},{1,2},{2,3},{3,0},{4,5},{5,6},{6,7},{7,4},{8,9},{9,10},{10,1... | collective-permute-start | bytes 2359304 | tf_op jit(solution)/shard_map/ppermute | solution.py:60
  117.1 13.2 %collective-permute-start.25 = (f32[768,256]{1,0:T(8,128)S(1)}, f32[768,256]{1,0:T(8,128)S(1)}, u32[]{:S(2)}, u32[]{:S(2)}) collective-permute-start(f32[768,256]{1,0:T(8,128)S(1)} %pad_maximum_fusion.3.refs_1_), channel_id=1, source_target_pairs={{0,3},{1,0},{2,1},{3,2},{4,7},{5,4},{6,5},{7,6},{8,11},{9,8},{10,9... | collective-permute-start | bytes 2359304 | tf_op jit(solution)/shard_map/ppermute | solution.py:60
  118.0 20.8 %collective-permute-start.24 = (f32[768,256]{1,0:T(8,128)S(1)}, f32[768,256]{1,0:T(8,128)S(1)}, u32[]{:S(2)}, u32[]{:S(2)}) collective-permute-start(f32[768,256]{1,0:T(8,128)S(1)} %pad_maximum_fusion.2.refs_0_), channel_id=1, source_target_pairs={{0,3},{1,0},{2,1},{3,2},{4,7},{5,4},{6,5},{7,6},{8,11},{9,8},{10,9... | collective-permute-start | bytes 2359304 | tf_op jit(solution)/shard_map/ppermute | solution.py:60
  119.3 19.4 %collective-permute-start.23 = (f32[768,256]{1,0:T(8,128)S(1)}, f32[768,256]{1,0:T(8,128)S(1)}, u32[]{:S(2)}, u32[]{:S(2)}) collective-permute-start(f32[768,256]{1,0:T(8,128)S(1)} %pad_maximum_fusion.3.refs_1_), channel_id=1, source_target_pairs={{0,1},{1,2},{2,3},{3,0},{4,5},{5,6},{6,7},{7,4},{8,9},{9,10},{10,1... | collective-permute-start | bytes 2359304 | tf_op jit(solution)/shard_map/ppermute | solution.py:60
  128.0 16.9 %collective-permute-start.26 = (f32[768,256]{1,0:T(8,128)S(1)}, f32[768,256]{1,0:T(8,128)S(1)}, u32[]{:S(2)}, u32[]{:S(2)}) collective-permute-start(f32[768,256]{1,0:T(8,128)S(1)} %collective-permute-done.22.refs_2_), channel_id=1, source_target_pairs={{0,1},{1,2},{2,3},{3,0},{4,5},{5,6},{6,7},{7,4},{8,9},{9,10},{10,1... | collective-permute-start | bytes 2359304 | tf_op jit(solution)/shard_map/ppermute | solution.py:60
  130.3 16.8 %collective-permute-start.27 = (f32[768,256]{1,0:T(8,128)S(1)}, f32[768,256]{1,0:T(8,128)S(1)}, u32[]{:S(2)}, u32[]{:S(2)}) collective-permute-start(f32[768,256]{1,0:T(8,128)S(1)} %collective-permute-done.25.refs_5_), channel_id=1, source_target_pairs={{0,3},{1,0},{2,1},{3,2},{4,7},{5,4},{6,5},{7,6},{8,11},{9,8},{10,9... | collective-permute-start | bytes 2359304 | tf_op jit(solution)/shard_map/ppermute | solution.py:60
  161.3 13.0 %collective-permute-start.31 = (f32[384,256]{1,0:T(8,128)S(1)}, f32[384,256]{1,0:T(8,128)S(1)}, u32[]{:S(2)}, u32[]{:S(2)}) collective-permute-start(f32[384,256]{1,0:T(8,128)S(1)} %fusion.17), channel_id=1, source_target_pairs={{0,32},{1,33},{2,34},{3,35},{4,36},{5,37},{6,38},{7,39},{8,40},{9,... | collective-permute-start | bytes 1179656 | tf_op jit(solution)/shard_map/ppermute | solution.py:60
  161.5 13.0 %collective-permute-start.35 = (f32[384,256]{1,0:T(8,128)S(1)}, f32[384,256]{1,0:T(8,128)S(1)}, u32[]{:S(2)}, u32[]{:S(2)}) collective-permute-start(f32[384,256]{1,0:T(8,128)S(1)} %fusion.10), channel_id=1, source_target_pairs={{0,224},{1,225},{2,226},{3,227},{4,228},{5,229},{6,230},{7,231},{8... | collective-permute-start | bytes 1179656 | tf_op jit(solution)/shard_map/ppermute | solution.py:60
  174.4 12.1 %collective-permute-start.33 = (f32[384,256]{1,0:T(8,128)S(1)}, f32[384,256]{1,0:T(8,128)S(1)}, u32[]{:S(2)}, u32[]{:S(2)}) collective-permute-start(f32[384,256]{1,0:T(8,128)S(1)} %add.220), channel_id=1, source_target_pairs={{0,32},{1,33},{2,34},{3,35},{4,36},{5,37},{6,38},{7,39},{8,40},{9,... | collective-permute-start | bytes 1179656 | tf_op jit(solution)/shard_map/ppermute | solution.py:60
  174.5 12.1 %collective-permute-start.36 = (f32[384,256]{1,0:T(8,128)S(1)}, f32[384,256]{1,0:T(8,128)S(1)}, u32[]{:S(2)}, u32[]{:S(2)}) collective-permute-start(f32[384,256]{1,0:T(8,128)S(1)} %add.224), channel_id=1, source_target_pairs={{0,224},{1,225},{2,226},{3,227},{4,228},{5,229},{6,230},{7,231},{8... | collective-permute-start | bytes 1179656 | tf_op jit(solution)/shard_map/ppermute | solution.py:60
  (20 other events, 195.8 us)

commit v2 on v1

--- a/solution.py
+++ b/solution.py
@@ -75,6 +75,15 @@
     )
 
 
+def by_fours(step):
+    def four(i, _):
+        for u in range(4):
+            step(i * 4 + u, 0)
+        return 0
+
+    lax.fori_loop(0, TILES_DEV // 4, four, 0)
+
+
 def plan_kernel(place, col, slot, mirror, count, listed, cls, nxt):
     z, c, p, q = place[0], place[1], place[2], place[3]
     for s in range(SEGMENTS + 1):
@@ -94,7 +103,7 @@
         nxt[seg] = nxt[seg] + 1
         return 0
 
-    lax.fori_loop(0, TILES_DEV, classify, 0)
+    by_fours(classify)
     start = jnp.int32(0)
     for s in range(SEGMENTS):
         n = nxt[s]
@@ -129,7 +138,7 @@
         listed[DEST + at] = v - seg * 64
         return 0
 
-    lax.fori_loop(0, TILES_DEV, place_tile, 0)
+    by_fours(place_tile)
 
 
 def plan(place, col, slot, mirror, count):
@@ -248,7 +257,7 @@
 
 
 def gather(state, meanwhile=None):
-    a, b, c = (send(state, in_plane(d, 0)) for d in (1, -1, 2))
+    c, a, b = (send(state, in_plane(d, 0)) for d in (2, 1, -1))
     a, b, c, meanwhile = lax.optimization_barrier((a, b, c, meanwhile))
     up, down = in_plane(1, 1), in_plane(-1, 1)
     top, low = jnp.concatenate([state, a], axis=0), jnp.concatenate([b, c], axis=0)

time: 200 us -> 199 us (level)
  Pallas kernels: 26.3 us -> 29.1 us
  waiting for transfers between devices: 111 us -> 109 us
    pallas_call x6, Pallas kernels: 14.7 us -> 17.5 us  [products(): pl.pallas_call(kernel, out_shape=tuple(outs), in_specs=[SMEM] + [VMEM] *...]
    ppermute x38, waiting for transfers between devices: 111 us -> 109 us  [send(): return lax.ppermute(value, AXES, pairs)]
  transfers between devices with their start and end apart: 38 -> 38, of which waited for: 20 -> 22; matrix products, arithmetic and copies ran while one was open for 2% -> 2% of each run, Pallas kernels for 11% -> 13%
where the time goes in v2:
time: 199 us; the launch traced here: 198 us
  waiting for transfers between devices  109 us (55%)
  starting transfers between devices  48.1 us (24%)
  Pallas kernels  29.1 us (15%)
  local copies, waits for them, and re-layouts  4.68 us (2%)
  other arithmetic  4.18 us (2%)
  matrix products  2.21 us (1%)
    ppermute x38, waiting for transfers between devices, send(): return lax.ppermute(value, AXES, pairs)  109 us
    ppermute x38, starting transfers between devices, send(): return lax.ppermute(value, AXES, pairs)  48.1 us
    pallas_call x6, Pallas kernels, products(): pl.pallas_call(kernel, out_shape=tuple(outs), in_specs=[SMEM] + [VMEM] *...  17.5 us
    pallas_call x1, Pallas kernels, plan(): pl.pallas_call(plan_kernel, out_shape=jax.ShapeDtypeStruct((LISTED,), jnp...  6.32 us
    pallas_call x1, Pallas kernels, degrees(): pl.pallas_call(degree_kernel, out_shape=jax.ShapeDtypeStruct((2 * NZ, 8,...  5.3 us
  transfers between devices with their start and end apart: 38, of which 22 were waited for; matrix products, arithmetic and copies ran while one was open for 2% of the time, Pallas kernels for 13%

profile of v2, /device:TPU:24, one launch (start us, length us, event | category | flops | bytes accessed | tf_op | source)
XLA Modules:
  0.0 198.3 jit_solution(15769353039555708245)
XLA Ops:
  7.6 6.3 %plan.1.listed = s32[656]{0:T(1024)} custom-call(s32[4]{0:T(128)} %pad_add_fusion.place, s32[96]{0:T(128)} %col.1, s32[96]{0:T(128)} %slot.1, s32[32]{0:T(128)} %reshape.43.mirror, s32[1]{0:T(128)S(6)} %copy.17.count), custom_call_target="tpu_custom_call" | custom-call | bytes 20000000 | tf_op jit(solution)/shard_map/plan/pallas_call | solution.py:145
  20.5 6.7 %collective-permute-done.3.refs_2_ = f32[768,256]{1,0:T(8,128)S(1)} collective-permute-done((f32[768,256]{1,0:T(8,128)S(1)}, f32[768,256]{1,0:T(8,128)S(1)}, u32[]{:S(2)}, u32[]{:S(2)}) %collective-permute-start.3) | collective-permute-done | bytes 786464 | tf_op jit(solution)/shard_map/ppermute | solution.py:60
  32.8 5.3 %degrees.1.degree = f32[16,8,128]{2,1,0:T(8,128)S(1)} custom-call(s32[656]{0:T(1024)S(1)} %copy-done.2, f32[96,128,128]{2,1,0:T(8,128)S(1)} %copy-done), custom_call_target="tpu_custom_call" | custom-call | flops 100000000 | bytes 20000000 | tf_op jit(solution)/shard_map/degrees/pallas_call | solution.py:181
  38.5 5.6 %collective-permute-done.7.refs_6_ = f32[768,256]{1,0:T(8,128)S(1)} collective-permute-done((f32[768,256]{1,0:T(8,128)S(1)}, f32[768,256]{1,0:T(8,128)S(1)}, u32[]{:S(2)}, u32[]{:S(2)}) %collective-permute-start.7) | collective-permute-done | bytes 786464 | tf_op jit(solution)/shard_map/ppermute | solution.py:60
  53.4 4.6 %late.2 = f32[10,392,256]{2,1,0:T(8,128)S(1)} custom-call(s32[656]{0:T(1024)S(1)} %copy-done.2, f32[96,128,128]{2,1,0:T(8,128)S(1)} %copy-done.1, f32[16,8,128]{2,1,0:T(8,128)S(1)} %degrees.1.degree, bf16[48,128,256]{2,1,0:T(8,128)(2,1)S(1)} %get-tuple-element.57.high, bf16[48,128,256]{2,1,0:T(8,128)(2,1)S(1)} %get-tuple-element.58.low), custom_call_target="tpu_custom_call" | custom-call | flops 5000000000 | bytes 20000000 | tf_op jit(solution)/shard_map/late/pallas_call | solution.py:247
  58.1 5.2 %collective-permute-done.10 = f32[392,256]{1,0:T(8,128)S(1)} collective-permute-done((f32[392,256]{1,0:T(8,128)S(1)}, f32[392,256]{1,0:T(8,128)S(1)}, u32[]{:S(2)}, u32[]{:S(2)}) %collective-permute-start.10) | collective-permute-done | bytes 401440 | tf_op jit(solution)/shard_map/ppermute | solution.py:60
  63.7 3.3 %collective-permute-start.16 = (f32[392,256]{1,0:T(8,128)S(1)}, f32[392,256]{1,0:T(8,128)S(1)}, u32[]{:S(2)}, u32[]{:S(2)}) collective-permute-start(f32[392,256]{1,0:T(8,128)S(1)} %fusion.2), channel_id=1, source_target_pairs={{0,224},{1,225},{2,226},{3,227},{4,228},{5,229},{6,230},{7,231},{8... | collective-permute-start | bytes 1204232 | tf_op jit(solution)/shard_map/ppermute | solution.py:60
  67.6 8.0 %collective-permute-done.12 = f32[392,256]{1,0:T(8,128)S(1)} collective-permute-done((f32[392,256]{1,0:T(8,128)S(1)}, f32[392,256]{1,0:T(8,128)S(1)}, u32[]{:S(2)}, u32[]{:S(2)}) %collective-permute-start.12) | collective-permute-done | bytes 401440 | tf_op jit(solution)/shard_map/ppermute | solution.py:60
  75.8 3.3 %collective-permute-start.17 = (f32[392,256]{1,0:T(8,128)S(1)}, f32[392,256]{1,0:T(8,128)S(1)}, u32[]{:S(2)}, u32[]{:S(2)}) collective-permute-start(f32[392,256]{1,0:T(8,128)S(1)} %add.196), channel_id=1, source_target_pairs={{0,224},{1,225},{2,226},{3,227},{4,228},{5,229},{6,230},{7,231},{8... | collective-permute-start | bytes 1204232 | tf_op jit(solution)/shard_map/ppermute | solution.py:60
  79.1 9.7 %collective-permute-done.14 = f32[392,256]{1,0:T(8,128)S(1)} collective-permute-done((f32[392,256]{1,0:T(8,128)S(1)}, f32[392,256]{1,0:T(8,128)S(1)}, u32[]{:S(2)}, u32[]{:S(2)}) %collective-permute-start.14) | collective-permute-done | bytes 401440 | tf_op jit(solution)/shard_map/ppermute | solution.py:60
  89.0 3.3 %collective-permute-start.18 = (f32[392,256]{1,0:T(8,128)S(1)}, f32[392,256]{1,0:T(8,128)S(1)}, u32[]{:S(2)}, u32[]{:S(2)}) collective-permute-start(f32[392,256]{1,0:T(8,128)S(1)} %add.197), channel_id=1, source_target_pairs={{0,224},{1,225},{2,226},{3,227},{4,228},{5,229},{6,230},{7,231},{8... | collective-permute-start | bytes 1204232 | tf_op jit(solution)/shard_map/ppermute | solution.py:60
  92.8 8.6 %collective-permute-done.15 = f32[392,256]{1,0:T(8,128)S(1)} collective-permute-done((f32[392,256]{1,0:T(8,128)S(1)}, f32[392,256]{1,0:T(8,128)S(1)}, u32[]{:S(2)}, u32[]{:S(2)}) %collective-permute-start.15) | collective-permute-done | bytes 401440 | tf_op jit(solution)/shard_map/ppermute | solution.py:60
  106.6 5.2 %collective-permute-done.21 = f32[384,256]{1,0:T(8,128)S(1)} collective-permute-done((f32[384,256]{1,0:T(8,128)S(1)}, f32[384,256]{1,0:T(8,128)S(1)}, u32[]{:S(2)}, u32[]{:S(2)}) %collective-permute-start.21) | collective-permute-done | bytes 393248 | tf_op jit(solution)/shard_map/ppermute | solution.py:60
  111.8 3.4 %collective-permute-done.20 = f32[384,256]{1,0:T(8,128)S(1)} collective-permute-done((f32[384,256]{1,0:T(8,128)S(1)}, f32[384,256]{1,0:T(8,128)S(1)}, u32[]{:S(2)}, u32[]{:S(2)}) %collective-permute-start.20) | collective-permute-done | bytes 393248 | tf_op jit(solution)/shard_map/ppermute | solution.py:60
  121.4 6.7 %collective-permute-done.22.refs_2_ = f32[768,256]{1,0:T(8,128)S(1)} collective-permute-done((f32[768,256]{1,0:T(8,128)S(1)}, f32[768,256]{1,0:T(8,128)S(1)}, u32[]{:S(2)}, u32[]{:S(2)}) %collective-permute-start.22) | collective-permute-done | bytes 786464 | tf_op jit(solution)/shard_map/ppermute | solution.py:60
  130.1 7.7 %collective-permute-done.24.refs_4_ = f32[768,256]{1,0:T(8,128)S(1)} collective-permute-done((f32[768,256]{1,0:T(8,128)S(1)}, f32[768,256]{1,0:T(8,128)S(1)}, u32[]{:S(2)}, u32[]{:S(2)}) %collective-permute-start.24) | collective-permute-done | bytes 786464 | tf_op jit(solution)/shard_map/ppermute | solution.py:60
  137.8 7.1 %collective-permute-done.26.refs_6_ = f32[768,256]{1,0:T(8,128)S(1)} collective-permute-done((f32[768,256]{1,0:T(8,128)S(1)}, f32[768,256]{1,0:T(8,128)S(1)}, u32[]{:S(2)}, u32[]{:S(2)}) %collective-permute-start.26) | collective-permute-done | bytes 786464 | tf_op jit(solution)/shard_map/ppermute | solution.py:60
  151.3 4.5 %late.3 = f32[10,384,256]{2,1,0:T(8,128)S(1)} custom-call(s32[656]{0:T(1024)S(1)} %copy-done.2, f32[96,128,128]{2,1,0:T(8,128)S(1)} %copy-done.1, f32[16,8,128]{2,1,0:T(8,128)S(1)} %degrees.1.degree, bf16[48,128,256]{2,1,0:T(8,128)(2,1)S(1)} %get-tuple-element.77.high, bf16[48,128,256]{2,1,0:T(8,128)(2,1)S(1)} %get-tuple-element.78.low), custom_call_target="tpu_custom_call" | custom-call | flops 5000000000 | bytes 20000000 | tf_op jit(solution)/shard_map/late/pallas_call | solution.py:247
  156.1 4.2 %collective-permute-done.29 = f32[384,256]{1,0:T(8,128)S(1)} collective-permute-done((f32[384,256]{1,0:T(8,128)S(1)}, f32[384,256]{1,0:T(8,128)S(1)}, u32[]{:S(2)}, u32[]{:S(2)}) %collective-permute-start.29) | collective-permute-done | bytes 393248 | tf_op jit(solution)/shard_map/ppermute | solution.py:60
  160.5 3.3 %collective-permute-start.35 = (f32[384,256]{1,0:T(8,128)S(1)}, f32[384,256]{1,0:T(8,128)S(1)}, u32[]{:S(2)}, u32[]{:S(2)}) collective-permute-start(f32[384,256]{1,0:T(8,128)S(1)} %fusion.10), channel_id=1, source_target_pairs={{0,224},{1,225},{2,226},{3,227},{4,228},{5,229},{6,230},{7,231},{8... | collective-permute-start | bytes 1179656 | tf_op jit(solution)/shard_map/ppermute | solution.py:60
  164.5 8.8 %collective-permute-done.31 = f32[384,256]{1,0:T(8,128)S(1)} collective-permute-done((f32[384,256]{1,0:T(8,128)S(1)}, f32[384,256]{1,0:T(8,128)S(1)}, u32[]{:S(2)}, u32[]{:S(2)}) %collective-permute-start.31) | collective-permute-done | bytes 393248 | tf_op jit(solution)/shard_map/ppermute | solution.py:60
  176.9 8.7 %collective-permute-done.33 = f32[384,256]{1,0:T(8,128)S(1)} collective-permute-done((f32[384,256]{1,0:T(8,128)S(1)}, f32[384,256]{1,0:T(8,128)S(1)}, u32[]{:S(2)}, u32[]{:S(2)}) %collective-permute-start.33) | collective-permute-done | bytes 393248 | tf_op jit(solution)/shard_map/ppermute | solution.py:60
  185.7 3.3 %collective-permute-start.37 = (f32[384,256]{1,0:T(8,128)S(1)}, f32[384,256]{1,0:T(8,128)S(1)}, u32[]{:S(2)}, u32[]{:S(2)}) collective-permute-start(f32[384,256]{1,0:T(8,128)S(1)} %add.225), channel_id=1, source_target_pairs={{0,224},{1,225},{2,226},{3,227},{4,228},{5,229},{6,230},{7,231},{8... | collective-permute-start | bytes 1179656 | tf_op jit(solution)/shard_map/ppermute | solution.py:60
  189.5 7.3 %collective-permute-done.34 = f32[384,256]{1,0:T(8,128)S(1)} collective-permute-done((f32[384,256]{1,0:T(8,128)S(1)}, f32[384,256]{1,0:T(8,128)S(1)}, u32[]{:S(2)}, u32[]{:S(2)}) %collective-permute-start.34) | collective-permute-done | bytes 393248 | tf_op jit(solution)/shard_map/ppermute | solution.py:60
  (110 shorter events, 57.2 us)
Async XLA Ops:
  0.0 14.0 %collective-permute-start.2 = (f32[384,256]{1,0:T(8,128)}, f32[384,256]{1,0:T(8,128)S(1)}, u32[]{:S(2)}, u32[]{:S(2)}) collective-permute-start(f32[384,256]{1,0:T(8,128)} %param.8), channel_id=1, source_target_pairs={{0,8},{1,9},{2,10},{3,11},{4,12},{5,13},{6,14},{7,15},{8,0},{9,1},... | collective-permute-start | bytes 1179656 | tf_op jit(solution)/shard_map/ppermute | solution.py:60
  15.1 12.1 %collective-permute-start.3 = (f32[768,256]{1,0:T(8,128)S(1)}, f32[768,256]{1,0:T(8,128)S(1)}, u32[]{:S(2)}, u32[]{:S(2)}) collective-permute-start(f32[768,256]{1,0:T(8,128)S(1)} %get-tuple-element.50.refs_0_), channel_id=1, source_target_pairs={{0,1},{1,2},{2,3},{3,0},{4,5},{5,6},{6,7},{7,4},{8,9},{9,10},{10,1... | collective-permute-start | bytes 2359304 | tf_op jit(solution)/shard_map/ppermute | solution.py:60
  16.8 13.2 %collective-permute-start.6 = (f32[768,256]{1,0:T(8,128)S(1)}, f32[768,256]{1,0:T(8,128)S(1)}, u32[]{:S(2)}, u32[]{:S(2)}) collective-permute-start(f32[768,256]{1,0:T(8,128)S(1)} %get-tuple-element.51.refs_1_), channel_id=1, source_target_pairs={{0,3},{1,0},{2,1},{3,2},{4,7},{5,4},{6,5},{7,6},{8,11},{9,8},{10,9... | collective-permute-start | bytes 2359304 | tf_op jit(solution)/shard_map/ppermute | solution.py:60
  17.2 21.2 %collective-permute-start.5 = (f32[768,256]{1,0:T(8,128)S(1)}, f32[768,256]{1,0:T(8,128)S(1)}, u32[]{:S(2)}, u32[]{:S(2)}) collective-permute-start(f32[768,256]{1,0:T(8,128)S(1)} %get-tuple-element.50.refs_0_), channel_id=1, source_target_pairs={{0,3},{1,0},{2,1},{3,2},{4,7},{5,4},{6,5},{7,6},{8,11},{9,8},{10,9... | collective-permute-start | bytes 2359304 | tf_op jit(solution)/shard_map/ppermute | solution.py:60
  18.0 20.4 %collective-permute-start.4 = (f32[768,256]{1,0:T(8,128)S(1)}, f32[768,256]{1,0:T(8,128)S(1)}, u32[]{:S(2)}, u32[]{:S(2)}) collective-permute-start(f32[768,256]{1,0:T(8,128)S(1)} %get-tuple-element.51.refs_1_), channel_id=1, source_target_pairs={{0,1},{1,2},{2,3},{3,0},{4,5},{5,6},{6,7},{7,4},{8,9},{9,10},{10,1... | collective-permute-start | bytes 2359304 | tf_op jit(solution)/shard_map/ppermute | solution.py:60
  27.2 16.9 %collective-permute-start.7 = (f32[768,256]{1,0:T(8,128)S(1)}, f32[768,256]{1,0:T(8,128)S(1)}, u32[]{:S(2)}, u32[]{:S(2)}) collective-permute-start(f32[768,256]{1,0:T(8,128)S(1)} %collective-permute-done.3.refs_2_), channel_id=1, source_target_pairs={{0,1},{1,2},{2,3},{3,0},{4,5},{5,6},{6,7},{7,4},{8,9},{9,10},{10,1... | collective-permute-start | bytes 2359304 | tf_op jit(solution)/shard_map/ppermute | solution.py:60
  30.0 16.8 %collective-permute-start.8 = (f32[768,256]{1,0:T(8,128)S(1)}, f32[768,256]{1,0:T(8,128)S(1)}, u32[]{:S(2)}, u32[]{:S(2)}) collective-permute-start(f32[768,256]{1,0:T(8,128)S(1)} %collective-permute-done.6.refs_5_), channel_id=1, source_target_pairs={{0,3},{1,0},{2,1},{3,2},{4,7},{5,4},{6,5},{7,6},{8,11},{9,8},{10,9... | collective-permute-start | bytes 2359304 | tf_op jit(solution)/shard_map/ppermute | solution.py:60
  51.3 12.0 %collective-permute-start.11 = (f32[2,392,256]{2,1,0:T(8,128)S(1)}, f32[2,392,256]{2,1,0:T(8,128)S(1)}, u32[]{:S(2)}, u32[]{:S(2)}) collective-permute-start(f32[2,392,256]{2,1,0:T(8,128)S(1)} %slice.186), channel_id=1, source_target_pairs={{0,16},{1,17},{2,18},{3,19},{4,20},{5,21},{6,22},{7,23},{8,24},{9,... | collective-permute-start | bytes 2408456 | tf_op jit(solution)/shard_map/ppermute | solution.py:60
  63.4 12.2 %collective-permute-start.12 = (f32[392,256]{1,0:T(8,128)S(1)}, f32[392,256]{1,0:T(8,128)S(1)}, u32[]{:S(2)}, u32[]{:S(2)}) collective-permute-start(f32[392,256]{1,0:T(8,128)S(1)} %fusion.9), channel_id=1, source_target_pairs={{0,32},{1,33},{2,34},{3,35},{4,36},{5,37},{6,38},{7,39},{8,40},{9,... | collective-permute-start | bytes 1204232 | tf_op jit(solution)/shard_map/ppermute | solution.py:60
  63.7 12.0 %collective-permute-start.16 = (f32[392,256]{1,0:T(8,128)S(1)}, f32[392,256]{1,0:T(8,128)S(1)}, u32[]{:S(2)}, u32[]{:S(2)}) collective-permute-start(f32[392,256]{1,0:T(8,128)S(1)} %fusion.2), channel_id=1, source_target_pairs={{0,224},{1,225},{2,226},{3,227},{4,228},{5,229},{6,230},{7,231},{8... | collective-permute-start | bytes 1204232 | tf_op jit(solution)/shard_map/ppermute | solution.py:60
  75.6 13.2 %collective-permute-start.14 = (f32[392,256]{1,0:T(8,128)S(1)}, f32[392,256]{1,0:T(8,128)S(1)}, u32[]{:S(2)}, u32[]{:S(2)}) collective-permute-start(f32[392,256]{1,0:T(8,128)S(1)} %add.192), channel_id=1, source_target_pairs={{0,32},{1,33},{2,34},{3,35},{4,36},{5,37},{6,38},{7,39},{8,40},{9,... | collective-permute-start | bytes 1204232 | tf_op jit(solution)/shard_map/ppermute | solution.py:60
  75.8 13.2 %collective-permute-start.17 = (f32[392,256]{1,0:T(8,128)S(1)}, f32[392,256]{1,0:T(8,128)S(1)}, u32[]{:S(2)}, u32[]{:S(2)}) collective-permute-start(f32[392,256]{1,0:T(8,128)S(1)} %add.196), channel_id=1, source_target_pairs={{0,224},{1,225},{2,226},{3,227},{4,228},{5,229},{6,230},{7,231},{8... | collective-permute-start | bytes 1204232 | tf_op jit(solution)/shard_map/ppermute | solution.py:60
  88.9 12.6 %collective-permute-start.15 = (f32[392,256]{1,0:T(8,128)S(1)}, f32[392,256]{1,0:T(8,128)S(1)}, u32[]{:S(2)}, u32[]{:S(2)}) collective-permute-start(f32[392,256]{1,0:T(8,128)S(1)} %add.193), channel_id=1, source_target_pairs={{0,32},{1,33},{2,34},{3,35},{4,36},{5,37},{6,38},{7,39},{8,40},{9,... | collective-permute-start | bytes 1204232 | tf_op jit(solution)/shard_map/ppermute | solution.py:60
  89.0 12.4 %collective-permute-start.18 = (f32[392,256]{1,0:T(8,128)S(1)}, f32[392,256]{1,0:T(8,128)S(1)}, u32[]{:S(2)}, u32[]{:S(2)}) collective-permute-start(f32[392,256]{1,0:T(8,128)S(1)} %add.197), channel_id=1, source_target_pairs={{0,224},{1,225},{2,226},{3,227},{4,228},{5,229},{6,230},{7,231},{8... | collective-permute-start | bytes 1204232 | tf_op jit(solution)/shard_map/ppermute | solution.py:60
  116.0 12.1 %collective-permute-start.22 = (f32[768,256]{1,0:T(8,128)S(1)}, f32[768,256]{1,0:T(8,128)S(1)}, u32[]{:S(2)}, u32[]{:S(2)}) collective-permute-start(f32[768,256]{1,0:T(8,128)S(1)} %pad_maximum_fusion.2.refs_0_), channel_id=1, source_target_pairs={{0,1},{1,2},{2,3},{3,0},{4,5},{5,6},{6,7},{7,4},{8,9},{9,10},{10,1... | collective-permute-start | bytes 2359304 | tf_op jit(solution)/shard_map/ppermute | solution.py:60
  116.1 13.3 %collective-permute-start.25 = (f32[768,256]{1,0:T(8,128)S(1)}, f32[768,256]{1,0:T(8,128)S(1)}, u32[]{:S(2)}, u32[]{:S(2)}) collective-permute-start(f32[768,256]{1,0:T(8,128)S(1)} %pad_maximum_fusion.3.refs_1_), channel_id=1, source_target_pairs={{0,3},{1,0},{2,1},{3,2},{4,7},{5,4},{6,5},{7,6},{8,11},{9,8},{10,9... | collective-permute-start | bytes 2359304 | tf_op jit(solution)/shard_map/ppermute | solution.py:60
  118.1 19.7 %collective-permute-start.24 = (f32[768,256]{1,0:T(8,128)S(1)}, f32[768,256]{1,0:T(8,128)S(1)}, u32[]{:S(2)}, u32[]{:S(2)}) collective-permute-start(f32[768,256]{1,0:T(8,128)S(1)} %pad_maximum_fusion.2.refs_0_), channel_id=1, source_target_pairs={{0,3},{1,0},{2,1},{3,2},{4,7},{5,4},{6,5},{7,6},{8,11},{9,8},{10,9... | collective-permute-start | bytes 2359304 | tf_op jit(solution)/shard_map/ppermute | solution.py:60
  118.4 19.4 %collective-permute-start.23 = (f32[768,256]{1,0:T(8,128)S(1)}, f32[768,256]{1,0:T(8,128)S(1)}, u32[]{:S(2)}, u32[]{:S(2)}) collective-permute-start(f32[768,256]{1,0:T(8,128)S(1)} %pad_maximum_fusion.3.refs_1_), channel_id=1, source_target_pairs={{0,1},{1,2},{2,3},{3,0},{4,5},{5,6},{6,7},{7,4},{8,9},{9,10},{10,1... | collective-permute-start | bytes 2359304 | tf_op jit(solution)/shard_map/ppermute | solution.py:60
  128.1 16.9 %collective-permute-start.26 = (f32[768,256]{1,0:T(8,128)S(1)}, f32[768,256]{1,0:T(8,128)S(1)}, u32[]{:S(2)}, u32[]{:S(2)}) collective-permute-start(f32[768,256]{1,0:T(8,128)S(1)} %collective-permute-done.22.refs_2_), channel_id=1, source_target_pairs={{0,1},{1,2},{2,3},{3,0},{4,5},{5,6},{6,7},{7,4},{8,9},{9,10},{10,1... | collective-permute-start | bytes 2359304 | tf_op jit(solution)/shard_map/ppermute | solution.py:60
  129.4 16.9 %collective-permute-start.27 = (f32[768,256]{1,0:T(8,128)S(1)}, f32[768,256]{1,0:T(8,128)S(1)}, u32[]{:S(2)}, u32[]{:S(2)}) collective-permute-start(f32[768,256]{1,0:T(8,128)S(1)} %collective-permute-done.25.refs_5_), channel_id=1, source_target_pairs={{0,3},{1,0},{2,1},{3,2},{4,7},{5,4},{6,5},{7,6},{8,11},{9,8},{10,9... | collective-permute-start | bytes 2359304 | tf_op jit(solution)/shard_map/ppermute | solution.py:60
  160.4 13.0 %collective-permute-start.31 = (f32[384,256]{1,0:T(8,128)S(1)}, f32[384,256]{1,0:T(8,128)S(1)}, u32[]{:S(2)}, u32[]{:S(2)}) collective-permute-start(f32[384,256]{1,0:T(8,128)S(1)} %fusion.17), channel_id=1, source_target_pairs={{0,32},{1,33},{2,34},{3,35},{4,36},{5,37},{6,38},{7,39},{8,40},{9,... | collective-permute-start | bytes 1179656 | tf_op jit(solution)/shard_map/ppermute | solution.py:60
  160.5 13.0 %collective-permute-start.35 = (f32[384,256]{1,0:T(8,128)S(1)}, f32[384,256]{1,0:T(8,128)S(1)}, u32[]{:S(2)}, u32[]{:S(2)}) collective-permute-start(f32[384,256]{1,0:T(8,128)S(1)} %fusion.10), channel_id=1, source_target_pairs={{0,224},{1,225},{2,226},{3,227},{4,228},{5,229},{6,230},{7,231},{8... | collective-permute-start | bytes 1179656 | tf_op jit(solution)/shard_map/ppermute | solution.py:60
  173.4 12.1 %collective-permute-start.33 = (f32[384,256]{1,0:T(8,128)S(1)}, f32[384,256]{1,0:T(8,128)S(1)}, u32[]{:S(2)}, u32[]{:S(2)}) collective-permute-start(f32[384,256]{1,0:T(8,128)S(1)} %add.220), channel_id=1, source_target_pairs={{0,32},{1,33},{2,34},{3,35},{4,36},{5,37},{6,38},{7,39},{8,40},{9,... | collective-permute-start | bytes 1179656 | tf_op jit(solution)/shard_map/ppermute | solution.py:60
  173.6 12.1 %collective-permute-start.36 = (f32[384,256]{1,0:T(8,128)S(1)}, f32[384,256]{1,0:T(8,128)S(1)}, u32[]{:S(2)}, u32[]{:S(2)}) collective-permute-start(f32[384,256]{1,0:T(8,128)S(1)} %add.224), channel_id=1, source_target_pairs={{0,224},{1,225},{2,226},{3,227},{4,228},{5,229},{6,230},{7,231},{8... | collective-permute-start | bytes 1179656 | tf_op jit(solution)/shard_map/ppermute | solution.py:60
  (20 other events, 195.0 us)
